TPU v7x, 128 devices: a whole 4x4x4 slice. The times are simulated.
128 devices in a mesh: group: 4 (over x_hi, core), blk: 32 (over x_lo, z, y).
Axes of the slice: x: 4 (x_hi: 2, x_lo: 2; x = x_hi * 2 + x_lo), y: 4, z: 4, core: 2. Of those that a mesh axis runs over, the one named last changes fastest.
Arguments:
- image: float32 [16384, 1024], P(('group', 'blk')), may hold values from -8 to 8
- text: float32 [16384, 1024], P(('group', 'blk')), may hold values from -8 to 8
- pair: int32 [16384], P(('group', 'blk')), may hold values from 0 to 16383, as said below
Outputs:
- row_loss: float32 [16384], P(('group', 'blk'))
- grad_image: float32 [16384, 1024], P(('group', 'blk'))
- grad_text: float32 [16384, 1024], P(('group', 'blk'))
Inputs may be any that keep to these rules, and one draw needn't show every extreme that they name: `pair`: row r of block b of group g pairs with text row r of block (b + k) mod 32 of the same group, with k drawn per row.
All inputs are finite; a program needn't handle non-finite values.
Results may differ from a plain program's by a relative error of at most 0.0077.
Values may be sent and summed in bfloat16 or wider, within the bound.
A program may use at most 128 MiB of HBM per device.

v0:
```python
import math

import jax
import jax.numpy as jnp
from jax import lax
from jax.sharding import PartitionSpec as P

score_gain = 2.5


def shifted(array, axis, by):
    length = lax.axis_size(axis)
    return lax.ppermute(array, axis, [(i, (i + by) % length) for i in range(length)])


def local(image, text, pair):
    row_count = image.shape[0]
    width = image.shape[1]
    blocks = lax.axis_size("blk")
    window_rows = blocks * row_count
    images_bf = image.astype(jnp.bfloat16)
    texts_bf = text.astype(jnp.bfloat16)
    own_texts = lax.all_gather(texts_bf, "blk", axis=0, tiled=True)
    prior_texts = shifted(own_texts, "group", 1)
    scaling = score_gain / math.sqrt(width)
    contract_cols = (((1,), (1,)), ((), ()))
    contract_rows = (((0,), (0,)), ((), ()))
    score_own = (
        lax.dot_general(images_bf, own_texts, contract_cols, preferred_element_type=jnp.float32)
        * scaling
    )
    score_prior = (
        lax.dot_general(images_bf, prior_texts, contract_cols, preferred_element_type=jnp.float32)
        * scaling
    )
    row_peak = jnp.maximum(jnp.max(score_own, axis=1), jnp.max(score_prior, axis=1))[:, None]
    row_total = jnp.sum(jnp.exp(score_own - row_peak), axis=1) + jnp.sum(
        jnp.exp(score_prior - row_peak), axis=1
    )
    row_lse = row_peak[:, 0] + jnp.log(row_total)
    local_pair = pair - lax.axis_index("group") * window_rows
    columns = lax.broadcasted_iota(jnp.int32, (row_count, window_rows), 1)
    matches = columns == local_pair[:, None]
    positive = jnp.sum(jnp.where(matches, score_own, 0.0), axis=1)
    row_loss = row_lse - positive
    weight_own = jnp.exp(score_own - row_lse[:, None]).astype(jnp.bfloat16)
    weight_prior = jnp.exp(score_prior - row_lse[:, None]).astype(jnp.bfloat16)
    paired_texts = jnp.take(own_texts, local_pair, axis=0).astype(jnp.float32)
    grad_image = jnp.dot(weight_own, own_texts, preferred_element_type=jnp.float32)
    grad_image = grad_image + jnp.dot(weight_prior, prior_texts, preferred_element_type=jnp.float32)
    grad_image = grad_image - paired_texts
    images_wide = images_bf.astype(jnp.float32)
    weight_part = weight_own
    total_term = lax.dot_general(
        weight_part, images_bf, contract_rows, preferred_element_type=jnp.float32
    )
    target = local_pair
    inside = jnp.logical_and(target >= 0, target < lax.axis_size("blk") * row_count)
    target = jnp.where(inside, target, lax.axis_size("blk") * row_count)
    chosen = (
        jnp.zeros((lax.axis_size("blk") * row_count, width), jnp.float32)
        .at[target]
        .add(images_wide, mode="drop")
    )
    own_summed = lax.psum_scatter(total_term - chosen, "blk", scatter_dimension=0, tiled=True)
    weight_part = weight_prior
    prior_summed = lax.psum_scatter(
        lax.dot_general(weight_part, images_bf, contract_rows, preferred_element_type=jnp.float32),
        "blk",
        scatter_dimension=0,
        tiled=True,
    )
    returned = shifted(prior_summed, "group", -1)
    grad_text = own_summed + returned
    return (row_loss, grad_image, grad_text)


def solution(mesh):
    in_specs = (P(("group", "blk"), None), P(("group", "blk"), None), P(("group", "blk")))
    out_specs = (P(("group", "blk")), P(("group", "blk"), None), P(("group", "blk"), None))
    return jax.shard_map(local, mesh=mesh, in_specs=in_specs, out_specs=out_specs, check_vma=False)
```

profile of v0, /device:TPU:0, one launch (start us, length us, event | category | flops | bytes accessed | tf_op | source)
XLA Modules:
  0.0 707.4 jit_solution(10204840247415868756)
XLA Ops:
  7.2 0.0 all-gather.2.cloned.1.call-start
  7.2 1.8 convert_element_type.19
  9.0 0.0 all-gather.2.cloned.1.call-update
  9.0 0.0 reduce-scatter.5.cloned.1.call-start
  9.1 170.9 %all-gather.2.cloned.1.call-done = bf16[4096,1024]{1,0:T(8,128)(2,1)} async-done(((bf16[128,1024]{1,0:T(8,128)(2,1)}), bf16[4096,1024]{1,0:T(8,128)(2,1)}) %all-gather.2.cloned.1.call-update) | async-done | bytes 8388624 | tf_op jit(solution)/shard_map/all_gather | solution.py:23
  180.0 0.0 collective-permute-start
  180.0 1.1 convert_element_type.18
  181.1 0.7 compare_select_fusion
  181.7 6.4 fusion.7
  188.1 86.6 %collective-permute-done = bf16[4096,1024]{1,0:T(8,128)(2,1)} collective-permute-done((bf16[4096,1024]{1,0:T(8,128)(2,1)}, bf16[4096,1024]{1,0:T(8,128)(2,1)}, u32[]{:S(2)}, u32[]{:S(2)}) %collective-permute-start) | collective-permute-done | bytes 8388640 | tf_op jit(solution)/shard_map/ppermute | solution.py:13
  274.7 6.4 fusion.8
  281.1 0.0 copy-start
  281.1 1.0 select_reduce_fusion
  282.0 0.5 fusion.6
  282.6 0.0 copy-done
  282.6 8.2 %fusion.5 = f32[4096,1024]{1,0:T(8,128)} fusion(bf16[128,1024]{1,0:T(8,128)(2,1)S(1)} %convert_element_type.18, f32[128,4096]{1,0:T(8,128)S(1)} %get-tuple-element.13, f32[128]{0:T(128)S(1)} %get-tuple-element.9), kind=kOutput, calls=%fused_computation.24 | convolution fusion | flops 1074790400 | bytes 19137024 | tf_op jit(solution)/shard_map/dot_general | solution.py:68
  290.8 0.0 copy-start.1
  290.8 0.0 reduce-scatter.5.cloned.1.call-update
  290.8 0.0 reduce-scatter.3.cloned.1.call-start
  290.9 1.0 copy-done.1
  291.8 8.5 %scatter_custom_fusion = f32[4096,1024]{1,0:T(8,128)} fusion(s32[128]{0:T(128)S(1)} %get-tuple-element.6, f32[]{:T(128)} %constant.11.clone.1, f32[128,1024]{1,0:T(8,128)S(1)} %copy-done.1), kind=kCustom, calls=%fused_computation.3 | custom fusion | flops 393216 | bytes 17301508 | tf_op jit(solution)/shard_map/scatter-add | solution.py:63
  300.4 14.1 %convolution_subtract_fusion = f32[4096,1024]{1,0:T(8,128)} fusion(f32[4096,1024]{1,0:T(8,128)} %scatter_custom_fusion, bf16[128,1024]{1,0:T(8,128)(2,1)S(1)} %convert_element_type.18, f32[128,4096]{1,0:T(8,128)S(1)} %get-tuple-element.11, f32[128]{0:T(128)S(1)} %get-tuple-element.9), kind=kOutput, calls=%fused_computation.2 | convolution fusion | flops 1078984704 | bytes 35914240 | tf_op jit(solution)/shard_map/dot_general | solution.py:54
  314.5 0.0 reduce-scatter.3.cloned.1.call-update
  314.6 5.6 gather_fusion
  320.2 4.8 fusion.4
  325.0 169.7 %reduce-scatter.5.cloned.1.call-done = f32[128,1024]{1,0:T(8,128)} async-done(((f32[4096,1024]{1,0:T(8,128)}), f32[128,1024]{1,0:T(8,128)}) %reduce-scatter.5.cloned.1.call-update) | async-done | bytes 524304 | tf_op jit(solution)/shard_map/reduce_scatter | solution.py:67
  494.7 0.0 collective-permute-start.1
  494.7 6.2 fusion.2
  500.8 198.1 %reduce-scatter.3.cloned.1.call-done = f32[128,1024]{1,0:T(8,128)} async-done(((f32[4096,1024]{1,0:T(8,128)}), f32[128,1024]{1,0:T(8,128)}) %reduce-scatter.3.cloned.1.call-update) | async-done | bytes 524304 | tf_op jit(solution)/shard_map/reduce_scatter | solution.py:65
  699.0 0.0 collective-permute-done.1
  699.0 1.9 add.43
  (4 shorter events, 0.0 us)
Async XLA Ops:
  7.2 172.8 %all-gather.2.cloned.1.call-start = ((), (), s32[]{:S(2)}) async-start(), calls=%async_computation.2 | async-start | bytes 8650752 | tf_op jit(solution)/shard_map/all_gather | solution.py:23
  9.0 485.7 %reduce-scatter.5.cloned.1.call-start = ((), (), s32[]{:S(2)}) async-start(), calls=%async_computation.4 | async-start | bytes 17301504 | tf_op jit(solution)/shard_map/reduce_scatter | solution.py:67
  180.0 94.7 %collective-permute-start = (bf16[4096,1024]{1,0:T(8,128)(2,1)}, bf16[4096,1024]{1,0:T(8,128)(2,1)}, u32[]{:S(2)}, u32[]{:S(2)}) collective-permute-start(bf16[4096,1024]{1,0:T(8,128)(2,1)} %all-gather.2.cloned.1.call-done), channel_id=1, source_target_pairs={{0,32},{32,64},{64,96},{96,0},{1,33},{33,65},{65,97},{97,1},{2,34}... | collective-permute-start | bytes 25165832 | tf_op jit(solution)/shard_map/ppermute | solution.py:13
  281.1 1.5 copy-start
  290.8 1.0 copy-start.1
  290.8 408.1 %reduce-scatter.3.cloned.1.call-start = ((), (), s32[]{:S(2)}) async-start(), calls=%async_computation.3 | async-start | bytes 17301504 | tf_op jit(solution)/shard_map/reduce_scatter | solution.py:65
  494.7 204.3 %collective-permute-start.1 = (f32[128,1024]{1,0:T(8,128)}, f32[128,1024]{1,0:T(8,128)S(1)}, u32[]{:S(2)}, u32[]{:S(2)}) collective-permute-start(f32[128,1024]{1,0:T(8,128)} %reduce-scatter.5.cloned.1.call-done), channel_id=1, source_target_pairs={{0,96},{32,0},{64,32},{96,64},{1,97},{33,1},{65,33},{97,65},{2,98}... | collective-permute-start | bytes 1572872 | tf_op jit(solution)/shard_map/ppermute | solution.py:13
Sparse Core Ops, SparseCore 0:
  10.2 169.7 all-gather.1
  290.9 203.6 reduce-scatter.4
  497.1 201.8 reduce-scatter.2
where the time goes:
time: 708 us; the launch traced here: 707 us
  waiting for transfers between devices  625 us (88%)
  matrix products  46 us (6%)
  other arithmetic  15.5 us (2%)
  between operations  13.8 us (2%)
    reduce_scatter x1, waiting for transfers between devices, local(): lax.psum_scatter(total_term - chosen, 'blk', scatter_dimension=0, tiled=T...  198 us
    all_gather x1, waiting for transfers between devices, local(): own_texts = lax.all_gather(texts_bf, 'blk', axis=0, tiled=True)  171 us
    reduce_scatter x1, waiting for transfers between devices, local(): lax.psum_scatter(lax.dot_general(weight_part, images_bf, contract_rows, p...  170 us
    ppermute x2, waiting for transfers between devices, shifted(): lax.ppermute(array, axis, [(i, (i + by) % length) for i in range(length)])  86.6 us
    dot_general x2, matrix products, local(): lax.dot_general(weight_part, images_bf, contract_rows, preferred_element_...  22.3 us
  transfers between devices with their start and end apart: 5, of which 4 were waited for; matrix products, arithmetic and copies ran while one was open for 7% of the time, Pallas kernels for 0%

commit v1 on v0

v1 whole, which is shorter than its diff:
```python
import functools
import math

import jax
import jax.numpy as jnp
from jax import lax
from jax.experimental import pallas as pl
from jax.experimental.pallas import tpu as pltpu
from jax.sharding import PartitionSpec as P

MESH = pl.DeviceIdType.MESH
score_gain = 2.5
CA = 512
NT = (((1,), (1,)), ((), ()))
TN = (((0,), (0,)), ((), ()))
NN = (((1,), (0,)), ((), ()))

OFFSET = (0, 3, 1, 2)
PLACE = [[OFFSET.index((OFFSET[a] + OFFSET[i]) % 4) for i in range(4)] for a in range(4)]
SEEN = [OFFSET.index((4 - OFFSET[a]) % 4) for a in range(4)]


def kernel(
    image_ref, text_ref, pair_ref, loss_ref, gi_ref, gt_ref,
    img, txt, pairs, est, peak, stats, lse_ref, wt,
    gif, gib, gtf, gtb, rp, rx, ra1, ra2, ra3, rb1, rb2, rt1, rt2,
    send_sem, recv_sem,
):
    g = lax.axis_index("group")
    b = lax.axis_index("blk")
    x, z, y = b // 16, (b // 4) % 4, b % 4
    px = 1 - x
    zs = [(z + o) % 4 for o in OFFSET]
    ys = [(y + o) % 4 for o in OFFSET]
    xs = [x, px]

    def at(xx, zz, yy):
        return (g, xx * 16 + zz * 4 + yy)

    def mates():
        return [(zi, xi) for zi in range(4) for xi in range(2) if (zi, xi) != (0, 0)]

    to_px = at(px, z, y)
    to_zm, to_zp = at(x, zs[1], y), at(x, zs[2], y)
    to_ym, to_yp = at(x, z, ys[1]), at(x, z, ys[2])
    next_g, last_g = (g + 1) % 4, (g + 3) % 4
    flip = lambda even: jnp.where(even, px, x)
    to_next = (next_g, flip(next_g % 2 == 0) * 16 + z * 4 + y)
    to_last = (last_g, flip(g % 2 == 0) * 16 + z * 4 + y)

    barrier = pltpu.get_barrier_semaphore()
    peers = [at(xs[xi], zs[zi], y) for zi, xi in mates()] + [to_ym, to_yp, to_next, to_last]
    for peer in peers:
        pl.semaphore_signal(barrier, inc=1, device_id=peer, device_id_type=MESH)

    img[0:128, :] = image_ref[...].astype(jnp.bfloat16)
    txt[0:128, :] = text_ref[...].astype(jnp.bfloat16)
    pairs[:, 0:128] = pair_ref[...]

    pl.semaphore_wait(barrier, len(peers))

    names = {}
    started = []

    def copy(name, src, dst, to):
        k = names.setdefault(name, len(names))
        return pltpu.make_async_remote_copy(
            src_ref=src, dst_ref=dst, send_sem=send_sem.at[k], recv_sem=recv_sem.at[k],
            device_id=to, device_id_type=MESH,
        )

    def send(name, src, dst, to):
        c = copy(name, src, dst, to)
        c.start()
        started.append(c)

    def arrived(name, dst):
        copy(name, dst, dst, to_px).wait_recv()

    def A(zi, xi):
        return img.at[zi * 256 + xi * 128 : zi * 256 + xi * 128 + 128, 0:CA]

    def B(zi, xi, lo=0, hi=128):
        return img.at[zi * 256 + xi * 128 + lo : zi * 256 + xi * 128 + hi, CA:1024]

    def T(s, lo=0, hi=128):
        return txt.at[s * 128 + lo : s * 128 + hi, :]

    send("T0", T(0), T(1), to_yp)
    send("T1", T(0), T(2), to_ym)
    send("A0", A(0, 0), A(0, 1), to_px)
    send("B0", B(0, 0), B(1, 0), to_zp)
    send("B1", B(0, 0), B(2, 0), to_zm)
    send("P0", T(0), T(4), to_next)
    send("A1", A(0, 0), A(1, 0), to_zp)
    send("A2", A(0, 0), A(2, 0), to_zm)
    send("B2", B(0, 0), B(0, 1), to_px)

    def chunk(zi, xi):
        return slice(zi * 256 + xi * 128, zi * 256 + xi * 128 + 128)

    for zi, xi in mates():
        send(f"I{zi}{xi}", pairs.at[:, 0:128], pairs.at[:, chunk(SEEN[zi], xi)], at(xs[xi], zs[zi], y))

    arrived("A0", A(0, 1))
    send("A3", A(0, 1), A(1, 1), to_zp)
    send("A4", A(0, 1), A(2, 1), to_zm)
    arrived("B0", B(1, 0))
    send("B3", B(1, 0, 0, 64), B(3, 0, 0, 64), to_zp)
    send("B5", B(1, 0), B(1, 1), to_px)
    arrived("B1", B(2, 0))
    send("B4", B(2, 0, 64, 128), B(3, 0, 64, 128), to_zm)
    send("B6", B(2, 0), B(2, 1), to_px)
    arrived("T0", T(1))
    send("T2", T(1, 0, 64), T(3, 0, 64), to_yp)
    send("P1", T(1), T(5), to_next)
    arrived("T1", T(2))
    send("T3", T(2, 64, 128), T(3, 64, 128), to_ym)
    send("P2", T(2), T(6), to_next)
    arrived("A1", A(1, 0))
    send("A5", A(1, 0), A(3, 0), to_zp)
    arrived("B3", B(3, 0, 0, 64))
    arrived("B4", B(3, 0, 64, 128))
    send("B7", B(3, 0), B(3, 1), to_px)
    arrived("A4", A(2, 1))
    send("A6", A(2, 1), A(3, 1), to_zm)
    arrived("T2", T(3, 0, 64))
    arrived("T3", T(3, 64, 128))
    send("P3", T(3), T(7), to_next)
    for zi, xi in mates():
        arrived(f"I{SEEN[zi]}{xi}", pairs.at[:, chunk(zi, xi)])

    scaling = score_gain / math.sqrt(1024)
    bases = [(g * 32 + x * 16 + z * 4 + ys[s]) * 128 for s in range(4)]
    row = lax.broadcasted_iota(jnp.int32, (128, 256), 0)

    def score(slot):
        cols = slice(slot * 256, slot * 256 + 256)
        top = jnp.full((1, 256), -jnp.inf, jnp.float32)
        for t in range(4):
            st = lax.dot_general(
                txt[t * 256 : t * 256 + 256, :], img[cols, :], NT, preferred_element_type=jnp.float32
            ) * scaling
            est[t * 256 : t * 256 + 256, cols] = st
            top = jnp.maximum(top, jnp.max(st, axis=0, keepdims=True))
        total = jnp.zeros((1, 256), jnp.float32)
        positive = jnp.zeros((1, 256), jnp.float32)
        wanted = pairs[:, cols]
        for t in range(8):
            st = est[t * 128 : t * 128 + 128, cols]
            if t < 4:
                match = row == wanted - bases[t]
                positive += jnp.sum(jnp.where(match, st, 0.0), axis=0, keepdims=True)
            e = jnp.exp(st - top)
            est[t * 128 : t * 128 + 128, cols] = e
            total += jnp.sum(e, axis=0, keepdims=True)
        peak[:, cols] = top
        stats[0, 0:1, cols] = top + jnp.log(total)
        stats[0, 1:2, cols] = positive

    for k in range(4):
        arrived(f"P{k}", T(4 + k))
    arrived("B2", B(0, 1))
    score(0)
    arrived("A3", A(1, 1))
    arrived("B5", B(1, 1))
    score(1)
    arrived("A2", A(2, 0))
    arrived("B6", B(2, 1))
    score(2)
    arrived("A5", A(3, 0))
    arrived("A6", A(3, 1))
    arrived("B7", B(3, 1))
    score(3)

    for zi, xi in mates():
        send(f"S{zi}{xi}", stats.at[0], stats.at[SEEN[zi] * 2 + xi], at(xs[xi], zs[zi], y))
    for zi, xi in mates():
        arrived(f"S{SEEN[zi]}{xi}", stats.at[zi * 2 + xi])

    def pieces(zi, xi, r):
        out = [[None, None] for _ in range(4)]
        for i in range(4):
            for j in range(2):
                out[PLACE[zi][i]][j ^ xi] = stats[zi * 2 + xi, r : r + 1, chunk(i, j)]
        return jnp.concatenate([out[i][j] for i in range(4) for j in range(2)], axis=1)

    everyone = [(zi, xi) for zi in range(4) for xi in range(2)]
    parts = [pieces(zi, xi, 0) for zi, xi in everyone]
    top = functools.reduce(jnp.maximum, parts)
    lse = top + jnp.log(sum(jnp.exp(p - top) for p in parts))
    lse_ref[...] = lse
    positive = sum(pieces(zi, xi, 1)[:, 0:128] for zi, xi in everyone)
    loss_ref[...] = lse[:, 0:128] - positive

    def weights(slot):
        cols = slice(slot * 256, slot * 256 + 256)
        factor = jnp.exp(peak[:, cols] - lse_ref[:, cols])
        wanted = pairs[:, cols]
        for t in range(8):
            w = est[t * 128 : t * 128 + 128, cols] * factor
            if t < 4:
                w = jnp.where(row == wanted - bases[t], w - 1.0, w)
            wt[t * 128 : t * 128 + 128, cols] = w.astype(jnp.bfloat16)

    for slot in range(4):
        weights(slot)

    def grad_text(slot):
        return lax.dot_general(
            wt[slot * 128 : slot * 128 + 128, :], img[...], NN, preferred_element_type=jnp.float32
        )

    def prior(slot):
        rows = slice((4 + slot) * 128, (5 + slot) * 128)
        gtb[rows, :] = grad_text(4 + slot).astype(jnp.bfloat16)
        send(f"q{slot}", gtb.at[rows, :], rp.at[slot], to_last)

    def own(slot):
        gtf[slot * 128 : slot * 128 + 128, :] = grad_text(slot)

    def gi_rows(slot, xi):
        return slice(slot * 256 + xi * 128, slot * 256 + xi * 128 + 128)

    def grad_image(slot):
        rows = slice(slot * 256, slot * 256 + 256)
        v = lax.dot_general(wt[:, rows], txt[...], TN, preferred_element_type=jnp.float32)
        gif[rows, :] = v
        gib[gi_rows(slot, 1), CA:1024] = v[128:256, CA:1024].astype(jnp.bfloat16)
        send(f"b{slot}", gib.at[gi_rows(slot, 1), CA:1024], rx.at[slot], to_px)

    def send_a(name, slot, xi, dst, to, more=None):
        rows = gi_rows(slot, xi)
        v = gif[rows, 0:CA]
        for m in more or []:
            v = v + m.astype(jnp.float32)
        gib[rows, 0:CA] = v.astype(jnp.bfloat16)
        send(name, gib.at[rows, 0:CA], dst, to)

    prior(3)
    grad_image(3)
    send_a("a0", 3, 0, ra1.at[0], to_zp)
    send_a("a1", 3, 1, ra1.at[1], to_zm)
    prior(1)
    prior(2)
    grad_image(1)
    send_a("a2", 1, 0, ra2.at[1, 0], to_zm)
    grad_image(2)
    send_a("a3", 2, 1, ra2.at[0, 1], to_zp)

    def b_sum(slot, lo, hi, more=None):
        rows = slice(slot * 256 + lo, slot * 256 + hi)
        v = gif[rows, CA:1024] + rx[slot, lo:hi, :].astype(jnp.float32)
        if more is not None:
            v = v + more.astype(jnp.float32)
        return rows, v

    def b_put(slot, lo, hi, more=None):
        rows, v = b_sum(slot, lo, hi, more)
        gib[rows, CA:1024] = v.astype(jnp.bfloat16)
        return gib.at[rows, CA:1024]

    arrived("b3", rx.at[3])
    send("b4", b_put(3, 0, 64), rb1.at[0], to_zp)
    send("b5", b_put(3, 64, 128), rb1.at[1], to_zm)
    arrived("a0", ra1.at[0])
    send_a("a4", 2, 0, ra2.at[0, 0], to_zp, [ra1[0]])
    arrived("a1", ra1.at[1])
    send_a("a5", 1, 1, ra2.at[1, 1], to_zm, [ra1[1]])
    prior(0)
    grad_image(0)
    own(3)

    def t_put(slot, lo, hi, more=None):
        v = gtf[slot * 128 + lo : slot * 128 + hi, :] + rp[slot, lo:hi, :].astype(jnp.float32)
        if more is not None:
            v = v + more.astype(jnp.float32)
        rows = slice(slot * 128 + lo, slot * 128 + hi)
        gtb[rows, :] = v.astype(jnp.bfloat16)
        return gtb.at[rows, :]

    arrived("q3", rp.at[3])
    send("t0", t_put(3, 0, 64), rt1.at[0], to_yp)
    send("t1", t_put(3, 64, 128), rt1.at[1], to_ym)
    own(1)
    own(2)
    arrived("b1", rx.at[1])
    arrived("b5", rb1.at[1])
    b_put(1, 0, 64)
    b_put(1, 64, 128, rb1[1])
    send("b6", gib.at[gi_rows(1, 0), CA:1024], rb2.at[1], to_zm)
    arrived("b2", rx.at[2])
    arrived("b4", rb1.at[0])
    b_put(2, 0, 64, rb1[0])
    b_put(2, 64, 128)
    send("b7", gib.at[gi_rows(2, 0), CA:1024], rb2.at[0], to_zp)
    arrived("q1", rp.at[1])
    arrived("t1", rt1.at[1])
    t_put(1, 0, 64)
    t_put(1, 64, 128, rt1[1])
    send("t2", gtb.at[128:256, :], rt2.at[1], to_ym)
    arrived("q2", rp.at[2])
    arrived("t0", rt1.at[0])
    t_put(2, 0, 64, rt1[0])
    t_put(2, 64, 128)
    send("t3", gtb.at[256:384, :], rt2.at[0], to_yp)
    own(0)
    arrived("a3", ra2.at[0, 1])
    arrived("a5", ra2.at[1, 1])
    send_a("a6", 0, 1, ra3, to_px, [ra2[0, 1], ra2[1, 1]])

    arrived("q0", rp.at[0])
    arrived("t2", rt2.at[1])
    arrived("t3", rt2.at[0])
    gt_ref[...] = (
        gtf[0:128, :] + rp[0].astype(jnp.float32)
        + rt2[0].astype(jnp.float32) + rt2[1].astype(jnp.float32)
    )
    arrived("b0", rx.at[0])
    arrived("b6", rb2.at[1])
    arrived("b7", rb2.at[0])
    gi_ref[:, CA:1024] = (
        gif[0:128, CA:1024] + rx[0].astype(jnp.float32)
        + rb2[0].astype(jnp.float32) + rb2[1].astype(jnp.float32)
    )
    arrived("a2", ra2.at[1, 0])
    arrived("a4", ra2.at[0, 0])
    arrived("a6", ra3)
    gi_ref[:, 0:CA] = (
        gif[0:128, 0:CA] + ra2[0, 0].astype(jnp.float32)
        + ra2[1, 0].astype(jnp.float32) + ra3[...].astype(jnp.float32)
    )
    for c in started:
        c.wait_send()


def local(image, text, pair):
    bf16, f32 = jnp.bfloat16, jnp.float32
    vmem = pl.BlockSpec(memory_space=pltpu.VMEM)
    CB = 1024 - CA
    loss, grad_image, grad_text = pl.pallas_call(
        kernel,
        out_shape=(
            jax.ShapeDtypeStruct((1, 128), f32),
            jax.ShapeDtypeStruct((128, 1024), f32),
            jax.ShapeDtypeStruct((128, 1024), f32),
        ),
        in_specs=[vmem] * 3,
        out_specs=(vmem,) * 3,
        scratch_shapes=[
            pltpu.VMEM((1024, 1024), bf16),
            pltpu.VMEM((1024, 1024), bf16),
            pltpu.VMEM((1, 1024), jnp.int32),
            pltpu.VMEM((1024, 1024), f32),
            pltpu.VMEM((1, 1024), f32),
            pltpu.VMEM((8, 2, 1024), f32),
            pltpu.VMEM((1, 1024), f32),
            pltpu.VMEM((1024, 1024), bf16),
            pltpu.VMEM((1024, 1024), f32),
            pltpu.VMEM((1024, 1024), bf16),
            pltpu.VMEM((512, 1024), f32),
            pltpu.VMEM((1024, 1024), bf16),
            pltpu.VMEM((4, 128, 1024), bf16),
            pltpu.VMEM((4, 128, CB), bf16),
            pltpu.VMEM((2, 128, CA), bf16),
            pltpu.VMEM((2, 2, 128, CA), bf16),
            pltpu.VMEM((128, CA), bf16),
            pltpu.VMEM((2, 64, CB), bf16),
            pltpu.VMEM((2, 128, CB), bf16),
            pltpu.VMEM((2, 64, 1024), bf16),
            pltpu.VMEM((2, 128, 1024), bf16),
            pltpu.SemaphoreType.DMA((64,)),
            pltpu.SemaphoreType.DMA((64,)),
        ],
        compiler_params=pltpu.CompilerParams(
            collective_id=0, has_side_effects=True, vmem_limit_bytes=56 * 1024 * 1024
        ),
        cost_estimate=pl.CostEstimate(
            flops=6 * 1024**3, bytes_accessed=2 * 1024 * 1024, transcendentals=1024 * 1024
        ),
    )(image, text, pair.reshape(1, 128))
    return loss.reshape(128), grad_image, grad_text


def solution(mesh):
    in_specs = (P(("group", "blk"), None), P(("group", "blk"), None), P(("group", "blk")))
    out_specs = (P(("group", "blk")), P(("group", "blk"), None), P(("group", "blk"), None))
    return jax.shard_map(local, mesh=mesh, in_specs=in_specs, out_specs=out_specs, check_vma=False)
```

time: 708 us -> 61.3 us (0.09)
  waiting for transfers between devices: 625 us -> 0 us
  Pallas kernels: 0 us -> 56.6 us
  matrix products: 46 us -> 0 us
  other arithmetic: 15.5 us -> 0 us
  between operations: 13.8 us -> 0.65 us
    reduce_scatter x2 -> x0, waiting for transfers between devices: 368 us -> none  [the longest x1 198 us: local(): lax.psum_scatter(total_term - chosen, 'blk', scatter_dimension=0, tiled=T...]
    all_gather x1 -> x0, waiting for transfers between devices: 171 us -> none  [local(): own_texts = lax.all_gather(texts_bf, 'blk', axis=0, tiled=True)]
    ppermute x2 -> x0, waiting for transfers between devices: 86.6 us -> none  [shifted(): lax.ppermute(array, axis, [(i, (i + by) % length) for i in range(length)])]
    pallas_call x0 -> x1, Pallas kernels: none -> 56.6 us  [local(): pl.pallas_call(kernel, out_shape=(jax.ShapeDtypeStruct((1, 128), f32), ja...]
    dot_general x6 -> x0, matrix products: 46 us -> none  [the longest x2 22.3 us: local(): lax.dot_general(weight_part, images_bf, contract_rows, preferred_element_...]
    scatter-add x1 -> x0, other arithmetic: 8.55 us -> none  [local(): chosen = jnp.zeros((lax.axis_size('blk') * row_count, width), jnp.float32...]
  transfers between devices with their start and end apart: 5 -> 0, of which waited for: 4 -> 0; matrix products, arithmetic and copies ran while one was open for 7% -> 0% of each run, Pallas kernels for 0% -> 0%
where the time goes in v1:
time: 61.3 us; the launch traced here: 61.1 us
  Pallas kernels  56.6 us (92%)
  local copies, waits for them, and re-layouts  3.91 us (6%)
  between operations  0.65 us (1%)
    pallas_call x1, Pallas kernels, local(): pl.pallas_call(kernel, out_shape=(jax.ShapeDtypeStruct((1, 128), f32), ja...  56.6 us
    unnamed x7, local copies, waits for them, and re-layouts  3.91 us

profile of v1, /device:TPU:0, one launch (start us, length us, event | category | flops | bytes accessed | tf_op | source)
XLA Modules:
  0.0 61.1 jit_solution(13536328696322941754)
XLA Ops:
  0.6 56.6 %shard_map.58 = (f32[1,128]{1,0:T(1,128)}, f32[128,1024]{1,0:T(8,128)}, f32[128,1024]{1,0:T(8,128)}) custom-call(f32[128,1024]{1,0:T(8,128)} %image_ref.1, f32[128,1024]{1,0:T(8,128)} %text_ref.1, s32[1,128]{1,0:T(1,128)} %bitcast.2), custom_call_target="tpu_custom_call" | custom-call | flops 6442450944 | bytes 2097152 | tf_op jit(solution)/shard_map/pallas_call | solution.py:341
  57.2 0.0 copy-start.1
  57.2 0.7 %copy-done.1 = f32[1,128]{1,0:T(1,128)S(1)} copy-done((f32[1,128]{1,0:T(1,128)S(1)}, f32[1,128]{1,0:T(1,128)}, u32[]{:S(2)}) %copy-start.1) | copy-done | bytes 536
  57.9 0.5 copy.9
  58.4 0.0 copy-start
  58.4 1.9 %copy.10 = f32[128,1024]{1,0:T(8,128)} copy(f32[128,1024]{1,0:T(8,128)} %get-tuple-element.13) | data formatting | bytes 1048576
  60.3 0.0 copy-done
  60.3 0.8 %copy.11 = f32[128,1024]{1,0:T(8,128)} copy(f32[128,1024]{1,0:T(8,128)S(1)} %copy-done) | data formatting | bytes 1048576
Async XLA Ops:
  57.2 0.7 %copy-start.1 = (f32[1,128]{1,0:T(1,128)S(1)}, f32[1,128]{1,0:T(1,128)}, u32[]{:S(2)}) copy-start(f32[1,128]{1,0:T(1,128)} %get-tuple-element.6) | copy-start | bytes 1540
  58.4 1.9 %copy-start = (f32[128,1024]{1,0:T(8,128)S(1)}, f32[128,1024]{1,0:T(8,128)}, u32[]{:S(2)}) copy-start(f32[128,1024]{1,0:T(8,128)} %get-tuple-element.14) | copy-start | bytes 1572868

commit v2 on v1

--- a/solution.py
+++ b/solution.py
@@ -22,9 +22,9 @@
 
 def kernel(
     image_ref, text_ref, pair_ref, loss_ref, gi_ref, gt_ref,
-    img, txt, pairs, est, peak, stats, lse_ref, wt,
+    img, txt, pairs, est, peak, stats, lse_ref, loss, wt,
     gif, gib, gtf, gtb, rp, rx, ra1, ra2, ra3, rb1, rb2, rt1, rt2,
-    send_sem, recv_sem,
+    send_sem, recv_sem, local_sem,
 ):
     g = lax.axis_index("group")
     b = lax.axis_index("blk")
@@ -53,9 +53,15 @@
     for peer in peers:
         pl.semaphore_signal(barrier, inc=1, device_id=peer, device_id_type=MESH)
 
-    img[0:128, :] = image_ref[...].astype(jnp.bfloat16)
-    txt[0:128, :] = text_ref[...].astype(jnp.bfloat16)
+    text_in = pltpu.make_async_copy(text_ref, gtf.at[0:128, :], local_sem.at[0])
+    image_in = pltpu.make_async_copy(image_ref, gif.at[0:128, :], local_sem.at[1])
+    text_in.start()
+    image_in.start()
     pairs[:, 0:128] = pair_ref[...]
+    text_in.wait()
+    txt[0:128, :] = gtf[0:128, :].astype(jnp.bfloat16)
+    image_in.wait()
+    img[0:128, :] = gif[0:128, :].astype(jnp.bfloat16)
 
     pl.semaphore_wait(barrier, len(peers))
 
@@ -86,12 +92,14 @@
     def T(s, lo=0, hi=128):
         return txt.at[s * 128 + lo : s * 128 + hi, :]
 
-    send("T0", T(0), T(1), to_yp)
-    send("T1", T(0), T(2), to_ym)
-    send("A0", A(0, 0), A(0, 1), to_px)
+    send("T0a", T(0, 0, 64), T(1, 0, 64), to_yp)
+    send("T1b", T(0, 64, 128), T(2, 64, 128), to_ym)
     send("B0", B(0, 0), B(1, 0), to_zp)
     send("B1", B(0, 0), B(2, 0), to_zm)
+    send("A0", A(0, 0), A(0, 1), to_px)
     send("P0", T(0), T(4), to_next)
+    send("T0b", T(0, 64, 128), T(1, 64, 128), to_yp)
+    send("T1a", T(0, 0, 64), T(2, 0, 64), to_ym)
     send("A1", A(0, 0), A(1, 0), to_zp)
     send("A2", A(0, 0), A(2, 0), to_zm)
     send("B2", B(0, 0), B(0, 1), to_px)
@@ -102,47 +110,22 @@
     for zi, xi in mates():
         send(f"I{zi}{xi}", pairs.at[:, 0:128], pairs.at[:, chunk(SEEN[zi], xi)], at(xs[xi], zs[zi], y))
 
-    arrived("A0", A(0, 1))
-    send("A3", A(0, 1), A(1, 1), to_zp)
-    send("A4", A(0, 1), A(2, 1), to_zm)
-    arrived("B0", B(1, 0))
-    send("B3", B(1, 0, 0, 64), B(3, 0, 0, 64), to_zp)
-    send("B5", B(1, 0), B(1, 1), to_px)
-    arrived("B1", B(2, 0))
-    send("B4", B(2, 0, 64, 128), B(3, 0, 64, 128), to_zm)
-    send("B6", B(2, 0), B(2, 1), to_px)
-    arrived("T0", T(1))
-    send("T2", T(1, 0, 64), T(3, 0, 64), to_yp)
-    send("P1", T(1), T(5), to_next)
-    arrived("T1", T(2))
-    send("T3", T(2, 64, 128), T(3, 64, 128), to_ym)
-    send("P2", T(2), T(6), to_next)
-    arrived("A1", A(1, 0))
-    send("A5", A(1, 0), A(3, 0), to_zp)
-    arrived("B3", B(3, 0, 0, 64))
-    arrived("B4", B(3, 0, 64, 128))
-    send("B7", B(3, 0), B(3, 1), to_px)
-    arrived("A4", A(2, 1))
-    send("A6", A(2, 1), A(3, 1), to_zm)
-    arrived("T2", T(3, 0, 64))
-    arrived("T3", T(3, 64, 128))
-    send("P3", T(3), T(7), to_next)
-    for zi, xi in mates():
-        arrived(f"I{SEEN[zi]}{xi}", pairs.at[:, chunk(zi, xi)])
-
     scaling = score_gain / math.sqrt(1024)
     bases = [(g * 32 + x * 16 + z * 4 + ys[s]) * 128 for s in range(4)]
     row = lax.broadcasted_iota(jnp.int32, (128, 256), 0)
 
-    def score(slot):
+    def score(slot, t):
         cols = slice(slot * 256, slot * 256 + 256)
-        top = jnp.full((1, 256), -jnp.inf, jnp.float32)
-        for t in range(4):
-            st = lax.dot_general(
-                txt[t * 256 : t * 256 + 256, :], img[cols, :], NT, preferred_element_type=jnp.float32
-            ) * scaling
-            est[t * 256 : t * 256 + 256, cols] = st
-            top = jnp.maximum(top, jnp.max(st, axis=0, keepdims=True))
+        st = lax.dot_general(
+            txt[t * 256 : t * 256 + 256, :], img[cols, :], NT, preferred_element_type=jnp.float32
+        ) * scaling
+        est[t * 256 : t * 256 + 256, cols] = st
+        top = jnp.max(st, axis=0, keepdims=True)
+        peak[:, cols] = top if t == 0 else jnp.maximum(peak[:, cols], top)
+
+    def local_stats(slot):
+        cols = slice(slot * 256, slot * 256 + 256)
+        top = peak[:, cols]
         total = jnp.zeros((1, 256), jnp.float32)
         positive = jnp.zeros((1, 256), jnp.float32)
         wanted = pairs[:, cols]
@@ -154,24 +137,70 @@
             e = jnp.exp(st - top)
             est[t * 128 : t * 128 + 128, cols] = e
             total += jnp.sum(e, axis=0, keepdims=True)
-        peak[:, cols] = top
         stats[0, 0:1, cols] = top + jnp.log(total)
         stats[0, 1:2, cols] = positive
 
-    for k in range(4):
-        arrived(f"P{k}", T(4 + k))
+    arrived("B0", B(1, 0))
+    send("B3", B(1, 0, 0, 64), B(3, 0, 0, 64), to_zp)
+    send("B5", B(1, 0), B(1, 1), to_px)
+    arrived("B1", B(2, 0))
+    send("B4", B(2, 0, 64, 128), B(3, 0, 64, 128), to_zm)
+    send("B6", B(2, 0), B(2, 1), to_px)
+    arrived("T0a", T(1, 0, 64))
+    send("T2", T(1, 0, 64), T(3, 0, 64), to_yp)
+    send("P1a", T(1, 0, 64), T(5, 0, 64), to_next)
+    arrived("T1b", T(2, 64, 128))
+    send("T3", T(2, 64, 128), T(3, 64, 128), to_ym)
+    send("P2b", T(2, 64, 128), T(6, 64, 128), to_next)
+    arrived("A0", A(0, 1))
+    send("A3", A(0, 1), A(1, 1), to_zp)
+    send("A4", A(0, 1), A(2, 1), to_zm)
+    arrived("T0b", T(1, 64, 128))
+    send("P1b", T(1, 64, 128), T(5, 64, 128), to_next)
+    arrived("T1a", T(2, 0, 64))
+    send("P2a", T(2, 0, 64), T(6, 0, 64), to_next)
+    for zi, xi in mates():
+        arrived(f"I{SEEN[zi]}{xi}", pairs.at[:, chunk(zi, xi)])
+    arrived("A1", A(1, 0))
+    send("A5", A(1, 0), A(3, 0), to_zp)
     arrived("B2", B(0, 1))
-    score(0)
+    score(0, 0)
+    arrived("B3", B(3, 0, 0, 64))
+    arrived("B4", B(3, 0, 64, 128))
+    send("B7", B(3, 0), B(3, 1), to_px)
+    arrived("T2", T(3, 0, 64))
+    send("P3a", T(3, 0, 64), T(7, 0, 64), to_next)
+    arrived("T3", T(3, 64, 128))
+    send("P3b", T(3, 64, 128), T(7, 64, 128), to_next)
+    score(0, 1)
+    arrived("A4", A(2, 1))
+    send("A6", A(2, 1), A(3, 1), to_zm)
     arrived("A3", A(1, 1))
     arrived("B5", B(1, 1))
-    score(1)
+    score(1, 0)
+    score(1, 1)
     arrived("A2", A(2, 0))
     arrived("B6", B(2, 1))
-    score(2)
+    score(2, 0)
+    score(2, 1)
+    arrived("P0", T(4))
+    arrived("P1a", T(5, 0, 64))
+    arrived("P1b", T(5, 64, 128))
+    for slot in range(3):
+        score(slot, 2)
+    arrived("P2a", T(6, 0, 64))
+    arrived("P2b", T(6, 64, 128))
+    arrived("P3a", T(7, 0, 64))
+    arrived("P3b", T(7, 64, 128))
+    for slot in range(3):
+        score(slot, 3)
+        local_stats(slot)
     arrived("A5", A(3, 0))
     arrived("A6", A(3, 1))
     arrived("B7", B(3, 1))
-    score(3)
+    for t in range(4):
+        score(3, t)
+    local_stats(3)
 
     for zi, xi in mates():
         send(f"S{zi}{xi}", stats.at[0], stats.at[SEEN[zi] * 2 + xi], at(xs[xi], zs[zi], y))
@@ -191,7 +220,7 @@
     lse = top + jnp.log(sum(jnp.exp(p - top) for p in parts))
     lse_ref[...] = lse
     positive = sum(pieces(zi, xi, 1)[:, 0:128] for zi, xi in everyone)
-    loss_ref[...] = lse[:, 0:128] - positive
+    loss[...] = lse[:, 0:128] - positive
 
     def weights(slot):
         cols = slice(slot * 256, slot * 256 + 256)
@@ -237,41 +266,15 @@
         gib[rows, 0:CA] = v.astype(jnp.bfloat16)
         send(name, gib.at[rows, 0:CA], dst, to)
 
-    prior(3)
-    grad_image(3)
-    send_a("a0", 3, 0, ra1.at[0], to_zp)
-    send_a("a1", 3, 1, ra1.at[1], to_zm)
-    prior(1)
-    prior(2)
-    grad_image(1)
-    send_a("a2", 1, 0, ra2.at[1, 0], to_zm)
-    grad_image(2)
-    send_a("a3", 2, 1, ra2.at[0, 1], to_zp)
-
     def b_sum(slot, lo, hi, more=None):
         rows = slice(slot * 256 + lo, slot * 256 + hi)
         v = gif[rows, CA:1024] + rx[slot, lo:hi, :].astype(jnp.float32)
         if more is not None:
             v = v + more.astype(jnp.float32)
-        return rows, v
-
-    def b_put(slot, lo, hi, more=None):
-        rows, v = b_sum(slot, lo, hi, more)
         gib[rows, CA:1024] = v.astype(jnp.bfloat16)
         return gib.at[rows, CA:1024]
 
-    arrived("b3", rx.at[3])
-    send("b4", b_put(3, 0, 64), rb1.at[0], to_zp)
-    send("b5", b_put(3, 64, 128), rb1.at[1], to_zm)
-    arrived("a0", ra1.at[0])
-    send_a("a4", 2, 0, ra2.at[0, 0], to_zp, [ra1[0]])
-    arrived("a1", ra1.at[1])
-    send_a("a5", 1, 1, ra2.at[1, 1], to_zm, [ra1[1]])
-    prior(0)
-    grad_image(0)
-    own(3)
-
-    def t_put(slot, lo, hi, more=None):
+    def t_sum(slot, lo, hi, more=None):
         v = gtf[slot * 128 + lo : slot * 128 + hi, :] + rp[slot, lo:hi, :].astype(jnp.float32)
         if more is not None:
             v = v + more.astype(jnp.float32)
@@ -279,74 +282,105 @@
         gtb[rows, :] = v.astype(jnp.bfloat16)
         return gtb.at[rows, :]
 
+    prior(3)
+    grad_image(3)
+    send_a("a1", 3, 1, ra1.at[1], to_zm)
+    send_a("a0", 3, 0, ra1.at[0], to_zp)
+    grad_image(2)
+    send_a("a3", 2, 1, ra2.at[0, 1], to_zp)
+    grad_image(1)
+    prior(1)
+    prior(2)
+    arrived("b3", rx.at[3])
+    send("b4", b_sum(3, 0, 64), rb1.at[0], to_zp)
+    send("b5", b_sum(3, 64, 128), rb1.at[1], to_zm)
+    arrived("a1", ra1.at[1])
+    send_a("a5", 1, 1, ra2.at[1, 1], to_zm, [ra1[1]])
+    arrived("a0", ra1.at[0])
+    send_a("a4", 2, 0, ra2.at[0, 0], to_zp, [ra1[0]])
+    send_a("a2", 1, 0, ra2.at[1, 0], to_zm)
+    grad_image(0)
+    prior(0)
+    own(3)
     arrived("q3", rp.at[3])
-    send("t0", t_put(3, 0, 64), rt1.at[0], to_yp)
-    send("t1", t_put(3, 64, 128), rt1.at[1], to_ym)
+    send("t0", t_sum(3, 0, 64), rt1.at[0], to_yp)
+    send("t1", t_sum(3, 64, 128), rt1.at[1], to_ym)
     own(1)
     own(2)
+    arrived("b2", rx.at[2])
+    b_sum(2, 64, 128)
+    arrived("b4", rb1.at[0])
+    b_sum(2, 0, 64, rb1[0])
+    send("b7", gib.at[gi_rows(2, 0), CA:1024], rb2.at[0], to_zp)
     arrived("b1", rx.at[1])
+    b_sum(1, 0, 64)
     arrived("b5", rb1.at[1])
-    b_put(1, 0, 64)
-    b_put(1, 64, 128, rb1[1])
+    b_sum(1, 64, 128, rb1[1])
     send("b6", gib.at[gi_rows(1, 0), CA:1024], rb2.at[1], to_zm)
-    arrived("b2", rx.at[2])
-    arrived("b4", rb1.at[0])
-    b_put(2, 0, 64, rb1[0])
-    b_put(2, 64, 128)
-    send("b7", gib.at[gi_rows(2, 0), CA:1024], rb2.at[0], to_zp)
     arrived("q1", rp.at[1])
+    t_sum(1, 0, 64)
     arrived("t1", rt1.at[1])
-    t_put(1, 0, 64)
-    t_put(1, 64, 128, rt1[1])
+    t_sum(1, 64, 128, rt1[1])
     send("t2", gtb.at[128:256, :], rt2.at[1], to_ym)
-    arrived("q2", rp.at[2])
-    arrived("t0", rt1.at[0])
-    t_put(2, 0, 64, rt1[0])
-    t_put(2, 64, 128)
-    send("t3", gtb.at[256:384, :], rt2.at[0], to_yp)
     own(0)
     arrived("a3", ra2.at[0, 1])
     arrived("a5", ra2.at[1, 1])
     send_a("a6", 0, 1, ra3, to_px, [ra2[0, 1], ra2[1, 1]])
-
+    arrived("q2", rp.at[2])
+    t_sum(2, 64, 128)
+    arrived("t0", rt1.at[0])
+    t_sum(2, 0, 64, rt1[0])
+    send("t3", gtb.at[256:384, :], rt2.at[0], to_yp)
+
+    loss_out = pltpu.make_async_copy(loss.at[0], loss_ref, local_sem.at[2])
+    loss_out.start()
+    arrived("b0", rx.at[0])
+    arrived("b6", rb2.at[1])
+    arrived("b7", rb2.at[0])
+    gif[0:128, CA:1024] = (
+        gif[0:128, CA:1024] + rx[0].astype(jnp.float32)
+        + rb2[0].astype(jnp.float32) + rb2[1].astype(jnp.float32)
+    )
     arrived("q0", rp.at[0])
     arrived("t2", rt2.at[1])
     arrived("t3", rt2.at[0])
-    gt_ref[...] = (
+    gtf[0:128, :] = (
         gtf[0:128, :] + rp[0].astype(jnp.float32)
         + rt2[0].astype(jnp.float32) + rt2[1].astype(jnp.float32)
     )
-    arrived("b0", rx.at[0])
-    arrived("b6", rb2.at[1])
-    arrived("b7", rb2.at[0])
-    gi_ref[:, CA:1024] = (
-        gif[0:128, CA:1024] + rx[0].astype(jnp.float32)
-        + rb2[0].astype(jnp.float32) + rb2[1].astype(jnp.float32)
-    )
+    text_out = pltpu.make_async_copy(gtf.at[0:128, :], gt_ref, local_sem.at[0])
+    text_out.start()
     arrived("a2", ra2.at[1, 0])
     arrived("a4", ra2.at[0, 0])
     arrived("a6", ra3)
-    gi_ref[:, 0:CA] = (
+    gif[0:128, 0:CA] = (
         gif[0:128, 0:CA] + ra2[0, 0].astype(jnp.float32)
         + ra2[1, 0].astype(jnp.float32) + ra3[...].astype(jnp.float32)
     )
+    image_out = pltpu.make_async_copy(gif.at[0:128, :], gi_ref, local_sem.at[1])
+    image_out.start()
     for c in started:
         c.wait_send()
+    loss_out.wait()
+    text_out.wait()
+    image_out.wait()
 
 
 def local(image, text, pair):
     bf16, f32 = jnp.bfloat16, jnp.float32
     vmem = pl.BlockSpec(memory_space=pltpu.VMEM)
+    hbm = pl.BlockSpec(memory_space=pltpu.HBM)
+    anywhere = pl.BlockSpec(memory_space=pl.ANY)
     CB = 1024 - CA
     loss, grad_image, grad_text = pl.pallas_call(
         kernel,
         out_shape=(
-            jax.ShapeDtypeStruct((1, 128), f32),
+            jax.ShapeDtypeStruct((128,), f32),
             jax.ShapeDtypeStruct((128, 1024), f32),
             jax.ShapeDtypeStruct((128, 1024), f32),
         ),
-        in_specs=[vmem] * 3,
-        out_specs=(vmem,) * 3,
+        in_specs=[hbm, hbm, vmem],
+        out_specs=(anywhere,) * 3,
         scratch_shapes=[
             pltpu.VMEM((1024, 1024), bf16),
             pltpu.VMEM((1024, 1024), bf16),
@@ -355,6 +389,7 @@
             pltpu.VMEM((1, 1024), f32),
             pltpu.VMEM((8, 2, 1024), f32),
             pltpu.VMEM((1, 1024), f32),
+            pltpu.VMEM((1, 128), f32),
             pltpu.VMEM((1024, 1024), bf16),
             pltpu.VMEM((1024, 1024), f32),
             pltpu.VMEM((1024, 1024), bf16),
@@ -369,17 +404,18 @@
             pltpu.VMEM((2, 128, CB), bf16),
             pltpu.VMEM((2, 64, 1024), bf16),
             pltpu.VMEM((2, 128, 1024), bf16),
-            pltpu.SemaphoreType.DMA((64,)),
-            pltpu.SemaphoreType.DMA((64,)),
+            pltpu.SemaphoreType.DMA((72,)),
+            pltpu.SemaphoreType.DMA((72,)),
+            pltpu.SemaphoreType.DMA((3,)),
         ],
         compiler_params=pltpu.CompilerParams(
-            collective_id=0, has_side_effects=True, vmem_limit_bytes=56 * 1024 * 1024
+            collective_id=0, has_side_effects=True, vmem_limit_bytes=52 * 1024 * 1024 + 640 * 1024
         ),
         cost_estimate=pl.CostEstimate(
             flops=6 * 1024**3, bytes_accessed=2 * 1024 * 1024, transcendentals=1024 * 1024
         ),
     )(image, text, pair.reshape(1, 128))
-    return loss.reshape(128), grad_image, grad_text
+    return loss, grad_image, grad_text
 
 
 def solution(mesh):

time: 61.3 us -> 54.7 us (0.89)
  Pallas kernels: 56.6 us -> 51 us
  local copies, waits for them, and re-layouts: 3.91 us -> 2.75 us
    pallas_call x1, Pallas kernels: 56.6 us -> 51 us  [local(): pl.pallas_call(kernel, out_shape=(jax.ShapeDtypeStruct((128,), f32), jax....]
    unnamed x7 -> x5, local copies, waits for them, and re-layouts: 3.91 us -> 2.75 us
where the time goes in v2:
time: 54.7 us; the launch traced here: 54.4 us
  Pallas kernels  51 us (93%)
  local copies, waits for them, and re-layouts  2.75 us (5%)
  between operations  0.65 us (1%)
    pallas_call x1, Pallas kernels, local(): pl.pallas_call(kernel, out_shape=(jax.ShapeDtypeStruct((128,), f32), jax....  51 us
    unnamed x5, local copies, waits for them, and re-layouts  2.75 us

profile of v2, /device:TPU:0, one launch (start us, length us, event | category | flops | bytes accessed | tf_op | source)
XLA Modules:
  0.0 54.4 jit_solution(14061808302905173012)
XLA Ops:
  0.6 0.0 copy-start
  0.6 0.6 %copy-done = s32[128]{0:T(128)S(1)} copy-done((s32[128]{0:T(128)S(1)}, s32[128]{0:T(128)}, u32[]{:S(2)}) %copy-start) | copy-done | bytes 536
  1.3 51.0 %shard_map.58 = (f32[128]{0:T(128)S(1)}, f32[128,1024]{1,0:T(8,128)S(1)}, f32[128,1024]{1,0:T(8,128)S(1)}) custom-call(f32[128,1024]{1,0:T(8,128)} %image_ref.1, f32[128,1024]{1,0:T(8,128)} %text_ref.1, s32[1,128]{1,0:T(1,128)S(1)} %bitcast.1), custom_call_target="tpu_custom_call" | custom-call | flops 6442450944 | bytes 2097152 | tf_op jit(solution)/shard_map/pallas_call | solution.py:375
  52.3 0.5 copy.9
  52.8 0.8 %copy.10 = f32[128,1024]{1,0:T(8,128)} copy(f32[128,1024]{1,0:T(8,128)S(1)} %get-tuple-element.7) | data formatting | bytes 1048576
  53.6 0.8 %copy.11 = f32[128,1024]{1,0:T(8,128)} copy(f32[128,1024]{1,0:T(8,128)S(1)} %get-tuple-element.8) | data formatting | bytes 1048576
Async XLA Ops:
  0.6 0.7 %copy-start = (s32[128]{0:T(128)S(1)}, s32[128]{0:T(128)}, u32[]{:S(2)}) copy-start(s32[128]{0:T(128)} %param.5) | copy-start | bytes 1540

commit v3 on v2

--- a/solution.py
+++ b/solution.py
@@ -22,8 +22,8 @@
 
 def kernel(
     image_ref, text_ref, pair_ref, loss_ref, gi_ref, gt_ref,
-    img, txt, pairs, est, peak, stats, lse_ref, loss, wt,
-    gif, gib, gtf, gtb, rp, rx, ra1, ra2, ra3, rb1, rb2, rt1, rt2,
+    img, txt, pairs, est, peak, stats, wt,
+    gif, gib, gtf, gtb, ru, rp, rx, ra1, ra2, ra3, rb1, rb2, rt1, rt2,
     send_sem, recv_sem, local_sem,
 ):
     g = lax.axis_index("group")
@@ -218,50 +218,56 @@
     parts = [pieces(zi, xi, 0) for zi, xi in everyone]
     top = functools.reduce(jnp.maximum, parts)
     lse = top + jnp.log(sum(jnp.exp(p - top) for p in parts))
-    lse_ref[...] = lse
     positive = sum(pieces(zi, xi, 1)[:, 0:128] for zi, xi in everyone)
-    loss[...] = lse[:, 0:128] - positive
-
-    def weights(slot):
-        cols = slice(slot * 256, slot * 256 + 256)
-        factor = jnp.exp(peak[:, cols] - lse_ref[:, cols])
-        wanted = pairs[:, cols]
-        for t in range(8):
-            w = est[t * 128 : t * 128 + 128, cols] * factor
+    loss_ref[...] = (lse[:, 0:128] - positive)[0]
+
+    factor = jnp.exp(peak[...] - lse)
+
+    def weights(t):
+        rows = slice(t * 128, t * 128 + 128)
+        for slot in range(4):
+            cols = slice(slot * 256, slot * 256 + 256)
+            w = est[rows, cols] * factor[:, cols]
             if t < 4:
-                w = jnp.where(row == wanted - bases[t], w - 1.0, w)
-            wt[t * 128 : t * 128 + 128, cols] = w.astype(jnp.bfloat16)
-
-    for slot in range(4):
-        weights(slot)
-
-    def grad_text(slot):
-        return lax.dot_general(
-            wt[slot * 128 : slot * 128 + 128, :], img[...], NN, preferred_element_type=jnp.float32
-        )
-
-    def prior(slot):
-        rows = slice((4 + slot) * 128, (5 + slot) * 128)
-        gtb[rows, :] = grad_text(4 + slot).astype(jnp.bfloat16)
-        send(f"q{slot}", gtb.at[rows, :], rp.at[slot], to_last)
-
-    def own(slot):
-        gtf[slot * 128 : slot * 128 + 128, :] = grad_text(slot)
-
-    def gi_rows(slot, xi):
-        return slice(slot * 256 + xi * 128, slot * 256 + xi * 128 + 128)
+                w = jnp.where(row == pairs[:, cols] - bases[t], w - 1.0, w)
+            wt[rows, cols] = w.astype(jnp.bfloat16)
+
+    def grad_text(slot, count=1):
+        rows = slice(slot * 128, (slot + count) * 128)
+        gtf[rows, :] = lax.dot_general(wt[rows, :], img[...], NN, preferred_element_type=jnp.float32)
+
+    def put(slot, lo, more=()):
+        rows = slice(slot * 128 + lo, slot * 128 + lo + 64)
+        v = gtf[rows, :]
+        for m in more:
+            v = v + m.astype(jnp.float32)
+        gtb[rows, :] = v.astype(jnp.bfloat16)
+        return gtb.at[rows, :]
+
+    def send_q(slot, lo, more=()):
+        send(f"q{slot}{lo}", put(4 + slot, lo, more), rp.at[slot, lo : lo + 64, :], to_last)
+
+    def send_t(slot, lo, more=()):
+        end, to = (1, to_ym) if slot == 1 else (0, to_yp)
+        more = [rp[slot, lo : lo + 64, :], *more]
+        send(f"t{slot}{lo}", put(slot, lo, more), rt2.at[end, lo : lo + 64, :], to)
+
+    def gi_rows(slot, xi, lo=0, hi=128):
+        return slice(slot * 256 + xi * 128 + lo, slot * 256 + xi * 128 + hi)
 
     def grad_image(slot):
         rows = slice(slot * 256, slot * 256 + 256)
         v = lax.dot_general(wt[:, rows], txt[...], TN, preferred_element_type=jnp.float32)
         gif[rows, :] = v
         gib[gi_rows(slot, 1), CA:1024] = v[128:256, CA:1024].astype(jnp.bfloat16)
+
+    def send_b(slot):
         send(f"b{slot}", gib.at[gi_rows(slot, 1), CA:1024], rx.at[slot], to_px)
 
-    def send_a(name, slot, xi, dst, to, more=None):
-        rows = gi_rows(slot, xi)
+    def send_a(name, slot, xi, dst, to, more=(), lo=0, hi=128):
+        rows = gi_rows(slot, xi, lo, hi)
         v = gif[rows, 0:CA]
-        for m in more or []:
+        for m in more:
             v = v + m.astype(jnp.float32)
         gib[rows, 0:CA] = v.astype(jnp.bfloat16)
         send(name, gib.at[rows, 0:CA], dst, to)
@@ -274,103 +280,110 @@
         gib[rows, CA:1024] = v.astype(jnp.bfloat16)
         return gib.at[rows, CA:1024]
 
-    def t_sum(slot, lo, hi, more=None):
-        v = gtf[slot * 128 + lo : slot * 128 + hi, :] + rp[slot, lo:hi, :].astype(jnp.float32)
-        if more is not None:
-            v = v + more.astype(jnp.float32)
-        rows = slice(slot * 128 + lo, slot * 128 + hi)
-        gtb[rows, :] = v.astype(jnp.bfloat16)
-        return gtb.at[rows, :]
-
-    prior(3)
+    weights(7)
+    grad_text(7)
+    send("u0", put(7, 0), ru.at[0], to_yp)
+    send("u1", put(7, 64), ru.at[1], to_ym)
+    weights(5)
+    weights(6)
+    grad_text(5, 2)
+    send_q(1, 0)
+    send_q(2, 64)
+    for t in range(5):
+        weights(t)
     grad_image(3)
     send_a("a1", 3, 1, ra1.at[1], to_zm)
     send_a("a0", 3, 0, ra1.at[0], to_zp)
+    send_b(3)
+    grad_text(3, 2)
+    send_q(0, 0)
+    send("t0", put(3, 0), rt1.at[0], to_yp)
+    send("t1", put(3, 64), rt1.at[1], to_ym)
     grad_image(2)
+    send_b(2)
     send_a("a3", 2, 1, ra2.at[0, 1], to_zp)
     grad_image(1)
-    prior(1)
-    prior(2)
-    arrived("b3", rx.at[3])
-    send("b4", b_sum(3, 0, 64), rb1.at[0], to_zp)
-    send("b5", b_sum(3, 64, 128), rb1.at[1], to_zm)
+    send_a("a2", 1, 0, ra2.at[1, 0], to_zm)
+    send_b(1)
+    arrived("u1", ru.at[1])
+    send_q(1, 64, [ru[1]])
+    arrived("u0", ru.at[0])
+    send_q(2, 0, [ru[0]])
+    send_q(0, 64)
+    grad_image(0)
+    send_b(0)
     arrived("a1", ra1.at[1])
-    send_a("a5", 1, 1, ra2.at[1, 1], to_zm, [ra1[1]])
+    for half in range(2):
+        lo = half * 64
+        send_a(
+            f"a5{half}", 1, 1, ra2.at[1, 1, lo : lo + 64, :], to_zm, [ra1[1, lo : lo + 64, :]], lo, lo + 64
+        )
+        if half == 0:
+            arrived("b3", rx.at[3])
+            send("b5", b_sum(3, 64, 128), rb1.at[1], to_zm)
+            send("b4", b_sum(3, 0, 64), rb1.at[0], to_zp)
     arrived("a0", ra1.at[0])
     send_a("a4", 2, 0, ra2.at[0, 0], to_zp, [ra1[0]])
-    send_a("a2", 1, 0, ra2.at[1, 0], to_zm)
-    grad_image(0)
-    prior(0)
-    own(3)
-    arrived("q3", rp.at[3])
-    send("t0", t_sum(3, 0, 64), rt1.at[0], to_yp)
-    send("t1", t_sum(3, 64, 128), rt1.at[1], to_ym)
-    own(1)
-    own(2)
+    grad_text(1, 2)
+    arrived("q10", rp.at[1, 0:64, :])
+    send_t(1, 0)
+    arrived("q264", rp.at[2, 64:128, :])
+    send_t(2, 64)
+    grad_text(0)
     arrived("b2", rx.at[2])
     b_sum(2, 64, 128)
     arrived("b4", rb1.at[0])
     b_sum(2, 0, 64, rb1[0])
     send("b7", gib.at[gi_rows(2, 0), CA:1024], rb2.at[0], to_zp)
+    arrived("t1", rt1.at[1])
+    arrived("q164", rp.at[1, 64:128, :])
+    send_t(1, 64, [rt1[1]])
+    arrived("a3", ra2.at[0, 1])
+    arrived("a50", ra2.at[1, 1, 0:64, :])
+    send_a("a60", 0, 1, ra3.at[0:64, :], to_px, [ra2[0, 1, 0:64, :], ra2[1, 1, 0:64, :]], 0, 64)
+    arrived("t0", rt1.at[0])
+    arrived("q20", rp.at[2, 0:64, :])
+    send_t(2, 0, [rt1[0]])
     arrived("b1", rx.at[1])
     b_sum(1, 0, 64)
     arrived("b5", rb1.at[1])
     b_sum(1, 64, 128, rb1[1])
     send("b6", gib.at[gi_rows(1, 0), CA:1024], rb2.at[1], to_zm)
-    arrived("q1", rp.at[1])
-    t_sum(1, 0, 64)
-    arrived("t1", rt1.at[1])
-    t_sum(1, 64, 128, rt1[1])
-    send("t2", gtb.at[128:256, :], rt2.at[1], to_ym)
-    own(0)
-    arrived("a3", ra2.at[0, 1])
-    arrived("a5", ra2.at[1, 1])
-    send_a("a6", 0, 1, ra3, to_px, [ra2[0, 1], ra2[1, 1]])
-    arrived("q2", rp.at[2])
-    t_sum(2, 64, 128)
-    arrived("t0", rt1.at[0])
-    t_sum(2, 0, 64, rt1[0])
-    send("t3", gtb.at[256:384, :], rt2.at[0], to_yp)
-
-    loss_out = pltpu.make_async_copy(loss.at[0], loss_ref, local_sem.at[2])
-    loss_out.start()
+    arrived("a51", ra2.at[1, 1, 64:128, :])
+    send_a("a61", 0, 1, ra3.at[64:128, :], to_px, [ra2[0, 1, 64:128, :], ra2[1, 1, 64:128, :]], 64, 128)
+
+    for lo in (0, 64):
+        arrived(f"q0{lo}", rp.at[0, lo : lo + 64, :])
+        arrived(f"t1{lo}", rt2.at[1, lo : lo + 64, :])
+        arrived(f"t2{lo}", rt2.at[0, lo : lo + 64, :])
+    gt_ref[...] = (
+        gtf[0:128, :] + rp[0].astype(jnp.float32)
+        + rt2[0].astype(jnp.float32) + rt2[1].astype(jnp.float32)
+    )
     arrived("b0", rx.at[0])
     arrived("b6", rb2.at[1])
     arrived("b7", rb2.at[0])
-    gif[0:128, CA:1024] = (
+    gi_ref[:, CA:1024] = (
         gif[0:128, CA:1024] + rx[0].astype(jnp.float32)
         + rb2[0].astype(jnp.float32) + rb2[1].astype(jnp.float32)
     )
-    arrived("q0", rp.at[0])
-    arrived("t2", rt2.at[1])
-    arrived("t3", rt2.at[0])
-    gtf[0:128, :] = (
-        gtf[0:128, :] + rp[0].astype(jnp.float32)
-        + rt2[0].astype(jnp.float32) + rt2[1].astype(jnp.float32)
-    )
-    text_out = pltpu.make_async_copy(gtf.at[0:128, :], gt_ref, local_sem.at[0])
-    text_out.start()
     arrived("a2", ra2.at[1, 0])
     arrived("a4", ra2.at[0, 0])
-    arrived("a6", ra3)
-    gif[0:128, 0:CA] = (
+    arrived("a60", ra3.at[0:64, :])
+    arrived("a61", ra3.at[64:128, :])
+    gi_ref[:, 0:CA] = (
         gif[0:128, 0:CA] + ra2[0, 0].astype(jnp.float32)
         + ra2[1, 0].astype(jnp.float32) + ra3[...].astype(jnp.float32)
     )
-    image_out = pltpu.make_async_copy(gif.at[0:128, :], gi_ref, local_sem.at[1])
-    image_out.start()
+    assert len(names) <= 96
     for c in started:
         c.wait_send()
-    loss_out.wait()
-    text_out.wait()
-    image_out.wait()
 
 
 def local(image, text, pair):
     bf16, f32 = jnp.bfloat16, jnp.float32
     vmem = pl.BlockSpec(memory_space=pltpu.VMEM)
     hbm = pl.BlockSpec(memory_space=pltpu.HBM)
-    anywhere = pl.BlockSpec(memory_space=pl.ANY)
     CB = 1024 - CA
     loss, grad_image, grad_text = pl.pallas_call(
         kernel,
@@ -380,7 +393,7 @@
             jax.ShapeDtypeStruct((128, 1024), f32),
         ),
         in_specs=[hbm, hbm, vmem],
-        out_specs=(anywhere,) * 3,
+        out_specs=(vmem,) * 3,
         scratch_shapes=[
             pltpu.VMEM((1024, 1024), bf16),
             pltpu.VMEM((1024, 1024), bf16),
@@ -388,14 +401,13 @@
             pltpu.VMEM((1024, 1024), f32),
             pltpu.VMEM((1, 1024), f32),
             pltpu.VMEM((8, 2, 1024), f32),
-            pltpu.VMEM((1, 1024), f32),
-            pltpu.VMEM((1, 128), f32),
             pltpu.VMEM((1024, 1024), bf16),
             pltpu.VMEM((1024, 1024), f32),
             pltpu.VMEM((1024, 1024), bf16),
-            pltpu.VMEM((512, 1024), f32),
+            pltpu.VMEM((1024, 1024), f32),
             pltpu.VMEM((1024, 1024), bf16),
-            pltpu.VMEM((4, 128, 1024), bf16),
+            pltpu.VMEM((2, 64, 1024), bf16),
+            pltpu.VMEM((3, 128, 1024), bf16),
             pltpu.VMEM((4, 128, CB), bf16),
             pltpu.VMEM((2, 128, CA), bf16),
             pltpu.VMEM((2, 2, 128, CA), bf16),
@@ -404,9 +416,9 @@
             pltpu.VMEM((2, 128, CB), bf16),
             pltpu.VMEM((2, 64, 1024), bf16),
             pltpu.VMEM((2, 128, 1024), bf16),
-            pltpu.SemaphoreType.DMA((72,)),
-            pltpu.SemaphoreType.DMA((72,)),
-            pltpu.SemaphoreType.DMA((3,)),
+            pltpu.SemaphoreType.DMA((96,)),
+            pltpu.SemaphoreType.DMA((96,)),
+            pltpu.SemaphoreType.DMA((2,)),
         ],
         compiler_params=pltpu.CompilerParams(
             collective_id=0, has_side_effects=True, vmem_limit_bytes=52 * 1024 * 1024 + 640 * 1024

time: 54.7 us -> 51.6 us (0.943)
  Pallas kernels: 51 us -> 47.8 us
    pallas_call x1, Pallas kernels: 51 us -> 47.8 us  [local(): pl.pallas_call(kernel, out_shape=(jax.ShapeDtypeStruct((128,), f32), jax....]
where the time goes in v3:
time: 51.6 us; the launch traced here: 51.2 us
  Pallas kernels  47.8 us (93%)
  local copies, waits for them, and re-layouts  2.75 us (5%)
  between operations  0.65 us (1%)
    pallas_call x1, Pallas kernels, local(): pl.pallas_call(kernel, out_shape=(jax.ShapeDtypeStruct((128,), f32), jax....  47.8 us
    unnamed x5, local copies, waits for them, and re-layouts  2.75 us

profile of v3, /device:TPU:0, one launch (start us, length us, event | category | flops | bytes accessed | tf_op | source)
XLA Modules:
  0.0 51.2 jit_solution(11366404800169210121)
XLA Ops:
  0.6 0.0 copy-start
  0.6 0.6 %copy-done = s32[128]{0:T(128)S(1)} copy-done((s32[128]{0:T(128)S(1)}, s32[128]{0:T(128)}, u32[]{:S(2)}) %copy-start) | copy-done | bytes 536
  1.3 47.8 %shard_map.58 = (f32[128]{0:T(128)S(1)}, f32[128,1024]{1,0:T(8,128)S(1)}, f32[128,1024]{1,0:T(8,128)S(1)}) custom-call(f32[128,1024]{1,0:T(8,128)} %image_ref.1, f32[128,1024]{1,0:T(8,128)} %text_ref.1, s32[1,128]{1,0:T(1,128)S(1)} %bitcast.1), custom_call_target="tpu_custom_call" | custom-call | flops 6442450944 | bytes 2097152 | tf_op jit(solution)/shard_map/pallas_call | solution.py:388
  49.1 0.5 %copy.9 = f32[128]{0:T(128)} copy(f32[128]{0:T(128)S(1)} %get-tuple-element.6) | data formatting | bytes 1024
  49.6 0.8 %copy.10 = f32[128,1024]{1,0:T(8,128)} copy(f32[128,1024]{1,0:T(8,128)S(1)} %get-tuple-element.7) | data formatting | bytes 1048576
  50.4 0.8 %copy.11 = f32[128,1024]{1,0:T(8,128)} copy(f32[128,1024]{1,0:T(8,128)S(1)} %get-tuple-element.8) | data formatting | bytes 1048576
Async XLA Ops:
  0.6 0.7 %copy-start = (s32[128]{0:T(128)S(1)}, s32[128]{0:T(128)}, u32[]{:S(2)}) copy-start(s32[128]{0:T(128)} %param.5) | copy-start | bytes 1540

commit v4 on v3

--- a/solution.py
+++ b/solution.py
@@ -21,7 +21,7 @@
 
 
 def kernel(
-    image_ref, text_ref, pair_ref, loss_ref, gi_ref, gt_ref,
+    image_ref, text_ref, pair_ref, loss_ref, gi_ref, gt_ref, gi_last_ref, gt_last_ref,
     img, txt, pairs, est, peak, stats, wt,
     gif, gib, gtf, gtb, ru, rp, rx, ra1, ra2, ra3, rb1, rb2, rt1, rt2,
     send_sem, recv_sem, local_sem,
@@ -83,8 +83,8 @@
     def arrived(name, dst):
         copy(name, dst, dst, to_px).wait_recv()
 
-    def A(zi, xi):
-        return img.at[zi * 256 + xi * 128 : zi * 256 + xi * 128 + 128, 0:CA]
+    def A(zi, xi, lo=0, hi=128):
+        return img.at[zi * 256 + xi * 128 + lo : zi * 256 + xi * 128 + hi, 0:CA]
 
     def B(zi, xi, lo=0, hi=128):
         return img.at[zi * 256 + xi * 128 + lo : zi * 256 + xi * 128 + hi, CA:1024]
@@ -98,17 +98,16 @@
     send("B1", B(0, 0), B(2, 0), to_zm)
     send("A0", A(0, 0), A(0, 1), to_px)
     send("P0", T(0), T(4), to_next)
+    def chunk(zi, xi):
+        return slice(zi * 256 + xi * 128, zi * 256 + xi * 128 + 128)
+
+    for zi, xi in mates():
+        send(f"I{zi}{xi}", pairs.at[:, 0:128], pairs.at[:, chunk(SEEN[zi], xi)], at(xs[xi], zs[zi], y))
     send("T0b", T(0, 64, 128), T(1, 64, 128), to_yp)
     send("T1a", T(0, 0, 64), T(2, 0, 64), to_ym)
     send("A1", A(0, 0), A(1, 0), to_zp)
     send("A2", A(0, 0), A(2, 0), to_zm)
     send("B2", B(0, 0), B(0, 1), to_px)
-
-    def chunk(zi, xi):
-        return slice(zi * 256 + xi * 128, zi * 256 + xi * 128 + 128)
-
-    for zi, xi in mates():
-        send(f"I{zi}{xi}", pairs.at[:, 0:128], pairs.at[:, chunk(SEEN[zi], xi)], at(xs[xi], zs[zi], y))
 
     scaling = score_gain / math.sqrt(1024)
     bases = [(g * 32 + x * 16 + z * 4 + ys[s]) * 128 for s in range(4)]
@@ -143,38 +142,41 @@
     arrived("B0", B(1, 0))
     send("B3", B(1, 0, 0, 64), B(3, 0, 0, 64), to_zp)
     send("B5", B(1, 0), B(1, 1), to_px)
+    arrived("A0", A(0, 1))
+    send("A40", A(0, 1, 0, 64), A(2, 1, 0, 64), to_zm)
     arrived("B1", B(2, 0))
     send("B4", B(2, 0, 64, 128), B(3, 0, 64, 128), to_zm)
     send("B6", B(2, 0), B(2, 1), to_px)
+    send("A41", A(0, 1, 64, 128), A(2, 1, 64, 128), to_zm)
     arrived("T0a", T(1, 0, 64))
+    send("P1a", T(1, 0, 64), T(5, 0, 64), to_next)
     send("T2", T(1, 0, 64), T(3, 0, 64), to_yp)
-    send("P1a", T(1, 0, 64), T(5, 0, 64), to_next)
     arrived("T1b", T(2, 64, 128))
+    send("P2b", T(2, 64, 128), T(6, 64, 128), to_next)
     send("T3", T(2, 64, 128), T(3, 64, 128), to_ym)
-    send("P2b", T(2, 64, 128), T(6, 64, 128), to_next)
-    arrived("A0", A(0, 1))
     send("A3", A(0, 1), A(1, 1), to_zp)
-    send("A4", A(0, 1), A(2, 1), to_zm)
     arrived("T0b", T(1, 64, 128))
     send("P1b", T(1, 64, 128), T(5, 64, 128), to_next)
     arrived("T1a", T(2, 0, 64))
     send("P2a", T(2, 0, 64), T(6, 0, 64), to_next)
-    for zi, xi in mates():
-        arrived(f"I{SEEN[zi]}{xi}", pairs.at[:, chunk(zi, xi)])
     arrived("A1", A(1, 0))
     send("A5", A(1, 0), A(3, 0), to_zp)
     arrived("B2", B(0, 1))
-    score(0, 0)
+    arrived("A40", A(2, 1, 0, 64))
+    send("A60", A(2, 1, 0, 64), A(3, 1, 0, 64), to_zm)
+    arrived("P1a", T(5, 0, 64))
+    send("U0", T(5, 0, 64), T(7, 0, 64), to_yp)
+    arrived("P2b", T(6, 64, 128))
+    send("U1", T(6, 64, 128), T(7, 64, 128), to_ym)
     arrived("B3", B(3, 0, 0, 64))
     arrived("B4", B(3, 0, 64, 128))
     send("B7", B(3, 0), B(3, 1), to_px)
+    arrived("A41", A(2, 1, 64, 128))
+    send("A61", A(2, 1, 64, 128), A(3, 1, 64, 128), to_zm)
     arrived("T2", T(3, 0, 64))
-    send("P3a", T(3, 0, 64), T(7, 0, 64), to_next)
     arrived("T3", T(3, 64, 128))
-    send("P3b", T(3, 64, 128), T(7, 64, 128), to_next)
+    score(0, 0)
     score(0, 1)
-    arrived("A4", A(2, 1))
-    send("A6", A(2, 1), A(3, 1), to_zm)
     arrived("A3", A(1, 1))
     arrived("B5", B(1, 1))
     score(1, 0)
@@ -184,19 +186,24 @@
     score(2, 0)
     score(2, 1)
     arrived("P0", T(4))
-    arrived("P1a", T(5, 0, 64))
     arrived("P1b", T(5, 64, 128))
-    for slot in range(3):
-        score(slot, 2)
+    score(0, 2)
+    score(1, 2)
+    score(2, 2)
     arrived("P2a", T(6, 0, 64))
-    arrived("P2b", T(6, 64, 128))
-    arrived("P3a", T(7, 0, 64))
-    arrived("P3b", T(7, 64, 128))
-    for slot in range(3):
-        score(slot, 3)
-        local_stats(slot)
+    arrived("U0", T(7, 0, 64))
+    arrived("U1", T(7, 64, 128))
+    score(0, 3)
+    score(1, 3)
+    score(2, 3)
+    for zi, xi in mates():
+        arrived(f"I{SEEN[zi]}{xi}", pairs.at[:, chunk(zi, xi)])
+    local_stats(0)
+    local_stats(1)
+    local_stats(2)
     arrived("A5", A(3, 0))
-    arrived("A6", A(3, 1))
+    arrived("A60", A(3, 1, 0, 64))
+    arrived("A61", A(3, 1, 64, 128))
     arrived("B7", B(3, 1))
     for t in range(4):
         score(3, t)
@@ -330,20 +337,20 @@
     arrived("q264", rp.at[2, 64:128, :])
     send_t(2, 64)
     grad_text(0)
+    arrived("t1", rt1.at[1])
+    arrived("q164", rp.at[1, 64:128, :])
+    send_t(1, 64, [rt1[1]])
     arrived("b2", rx.at[2])
     b_sum(2, 64, 128)
+    arrived("t0", rt1.at[0])
+    arrived("q20", rp.at[2, 0:64, :])
+    send_t(2, 0, [rt1[0]])
+    arrived("a3", ra2.at[0, 1])
+    arrived("a50", ra2.at[1, 1, 0:64, :])
+    send_a("a60", 0, 1, ra3.at[0:64, :], to_px, [ra2[0, 1, 0:64, :], ra2[1, 1, 0:64, :]], 0, 64)
     arrived("b4", rb1.at[0])
     b_sum(2, 0, 64, rb1[0])
     send("b7", gib.at[gi_rows(2, 0), CA:1024], rb2.at[0], to_zp)
-    arrived("t1", rt1.at[1])
-    arrived("q164", rp.at[1, 64:128, :])
-    send_t(1, 64, [rt1[1]])
-    arrived("a3", ra2.at[0, 1])
-    arrived("a50", ra2.at[1, 1, 0:64, :])
-    send_a("a60", 0, 1, ra3.at[0:64, :], to_px, [ra2[0, 1, 0:64, :], ra2[1, 1, 0:64, :]], 0, 64)
-    arrived("t0", rt1.at[0])
-    arrived("q20", rp.at[2, 0:64, :])
-    send_t(2, 0, [rt1[0]])
     arrived("b1", rx.at[1])
     b_sum(1, 0, 64)
     arrived("b5", rb1.at[1])
@@ -357,24 +364,24 @@
         arrived(f"t1{lo}", rt2.at[1, lo : lo + 64, :])
         arrived(f"t2{lo}", rt2.at[0, lo : lo + 64, :])
     gt_ref[...] = (
-        gtf[0:128, :] + rp[0].astype(jnp.float32)
-        + rt2[0].astype(jnp.float32) + rt2[1].astype(jnp.float32)
+        gtf[0:128, :] + rp[0].astype(jnp.float32) + rt2[0].astype(jnp.float32)
     )
+    gt_last_ref[...] = rt2[1]
     arrived("b0", rx.at[0])
     arrived("b6", rb2.at[1])
     arrived("b7", rb2.at[0])
     gi_ref[:, CA:1024] = (
-        gif[0:128, CA:1024] + rx[0].astype(jnp.float32)
-        + rb2[0].astype(jnp.float32) + rb2[1].astype(jnp.float32)
+        gif[0:128, CA:1024] + rx[0].astype(jnp.float32) + rb2[0].astype(jnp.float32)
     )
+    gi_last_ref[:, CA:1024] = rb2[1]
     arrived("a2", ra2.at[1, 0])
     arrived("a4", ra2.at[0, 0])
     arrived("a60", ra3.at[0:64, :])
     arrived("a61", ra3.at[64:128, :])
     gi_ref[:, 0:CA] = (
-        gif[0:128, 0:CA] + ra2[0, 0].astype(jnp.float32)
-        + ra2[1, 0].astype(jnp.float32) + ra3[...].astype(jnp.float32)
+        gif[0:128, 0:CA] + ra2[0, 0].astype(jnp.float32) + ra2[1, 0].astype(jnp.float32)
     )
+    gi_last_ref[:, 0:CA] = ra3[...]
     assert len(names) <= 96
     for c in started:
         c.wait_send()
@@ -385,15 +392,17 @@
     vmem = pl.BlockSpec(memory_space=pltpu.VMEM)
     hbm = pl.BlockSpec(memory_space=pltpu.HBM)
     CB = 1024 - CA
-    loss, grad_image, grad_text = pl.pallas_call(
+    loss, grad_image, grad_text, image_last, text_last = pl.pallas_call(
         kernel,
         out_shape=(
             jax.ShapeDtypeStruct((128,), f32),
             jax.ShapeDtypeStruct((128, 1024), f32),
             jax.ShapeDtypeStruct((128, 1024), f32),
+            jax.ShapeDtypeStruct((128, 1024), bf16),
+            jax.ShapeDtypeStruct((128, 1024), bf16),
         ),
         in_specs=[hbm, hbm, vmem],
-        out_specs=(vmem,) * 3,
+        out_specs=(vmem,) * 5,
         scratch_shapes=[
             pltpu.VMEM((1024, 1024), bf16),
             pltpu.VMEM((1024, 1024), bf16),
@@ -421,13 +430,13 @@
             pltpu.SemaphoreType.DMA((2,)),
         ],
         compiler_params=pltpu.CompilerParams(
-            collective_id=0, has_side_effects=True, vmem_limit_bytes=52 * 1024 * 1024 + 640 * 1024
+            collective_id=0, has_side_effects=True, vmem_limit_bytes=52 * 1024 * 1024 + 128 * 1024
         ),
         cost_estimate=pl.CostEstimate(
             flops=6 * 1024**3, bytes_accessed=2 * 1024 * 1024, transcendentals=1024 * 1024
         ),
     )(image, text, pair.reshape(1, 128))
-    return loss, grad_image, grad_text
+    return loss, grad_image + image_last.astype(f32), grad_text + text_last.astype(f32)
 
 
 def solution(mesh):

time: 51.6 us -> 50.6 us (0.981)
  local copies, waits for them, and re-layouts: 2.75 us -> 1.16 us
  other arithmetic: 0 us -> 1.1 us
  Pallas kernels: 47.8 us -> 46.9 us
    unnamed x5 -> x3, local copies, waits for them, and re-layouts: 2.75 us -> 1.16 us
    add x0 -> x1, other arithmetic: none -> 1.1 us  [local(): grad_text + text_last.astype(f32)]
    pallas_call x1, Pallas kernels: 47.8 us -> 46.9 us  [local(): pl.pallas_call(kernel, out_shape=(jax.ShapeDtypeStruct((128,), f32), jax....]
where the time goes in v4:
time: 50.6 us; the launch traced here: 49.8 us
  Pallas kernels  46.9 us (93%)
  local copies, waits for them, and re-layouts  1.16 us (2%)
  other arithmetic  1.1 us (2%)
  between operations  0.65 us (1%)
    pallas_call x1, Pallas kernels, local(): pl.pallas_call(kernel, out_shape=(jax.ShapeDtypeStruct((128,), f32), jax....  46.9 us
    unnamed x3, local copies, waits for them, and re-layouts  1.16 us
    add x1, other arithmetic, local(): grad_text + text_last.astype(f32)  1.1 us

profile of v4, /device:TPU:0, one launch (start us, length us, event | category | flops | bytes accessed | tf_op | source)
XLA Modules:
  0.0 49.8 jit_solution(55232751124258896)
XLA Ops:
  0.6 0.0 copy-start
  0.6 0.6 %copy-done = s32[128]{0:T(128)S(1)} copy-done((s32[128]{0:T(128)S(1)}, s32[128]{0:T(128)}, u32[]{:S(2)}) %copy-start) | copy-done | bytes 536
  1.3 46.9 %shard_map.58 = (f32[128]{0:T(128)S(1)}, f32[128,1024]{1,0:T(8,128)S(1)}, f32[128,1024]{1,0:T(8,128)S(1)}, bf16[128,1024]{1,0:T(8,128)(2,1)S(1)}, bf16[128,1024]{1,0:T(8,128)(2,1)S(1)}) custom-call(f32[128,1024]{1,0:T(8,128)} %image_ref.1, f32[128,1024]{1,0:T(8,128)} %text_ref.1, s32[1,128]{1,0:T(1,128)S(1)} %bitcast.1), custom_call_target="tpu_custom_call" | custom-call | flops 6442450944 | bytes 2097152 | tf_op jit(solution)/shard_map/pallas_call | solution.py:395
  48.2 1.1 %convert_add_fusion = (f32[128,1024]{1,0:T(8,128)}, f32[128,1024]{1,0:T(8,128)}) fusion(f32[128,1024]{1,0:T(8,128)S(1)} %get-tuple-element.11, bf16[128,1024]{1,0:T(8,128)(2,1)S(1)} %get-tuple-element.12, f32[128,1024]{1,0:T(8,128)S(1)} %get-tuple-element.9, bf16[128,1024]{1,0:T(8,128)(2,1)S(1)} %get-tuple-element.10), kind=kLoop, calls=%fused_computation | loop fusion | flops 524288 | bytes 2621440 | tf_op jit(solution)/shard_map/add | solution.py:439
  49.3 0.5 %copy.7 = f32[128]{0:T(128)} copy(f32[128]{0:T(128)S(1)} %get-tuple-element.18) | data formatting | bytes 1024
Async XLA Ops:
  0.6 0.7 %copy-start = (s32[128]{0:T(128)S(1)}, s32[128]{0:T(128)}, u32[]{:S(2)}) copy-start(s32[128]{0:T(128)} %param.5) | copy-start | bytes 1540

commit v5 on v4

--- a/solution.py
+++ b/solution.py
@@ -23,7 +23,7 @@
 def kernel(
     image_ref, text_ref, pair_ref, loss_ref, gi_ref, gt_ref, gi_last_ref, gt_last_ref,
     img, txt, pairs, est, peak, stats, wt,
-    gif, gib, gtf, gtb, ru, rp, rx, ra1, ra2, ra3, rb1, rb2, rt1, rt2,
+    ebf, chosen, across, gis, gif, gib, gtf, gtb, ru, rp, rx, ra1, ra2, ra3, rb1, rb2, rt1, rt2,
     send_sem, recv_sem, local_sem,
 ):
     g = lax.axis_index("group")
@@ -79,6 +79,10 @@
         c = copy(name, src, dst, to)
         c.start()
         started.append(c)
+
+    def settle(keep):
+        while len(started) > keep:
+            started.pop(0).wait_send()
 
     def arrived(name, dst):
         copy(name, dst, dst, to_px).wait_recv()
@@ -133,8 +137,10 @@
             if t < 4:
                 match = row == wanted - bases[t]
                 positive += jnp.sum(jnp.where(match, st, 0.0), axis=0, keepdims=True)
+                chosen[t * 128 : t * 128 + 128, cols] = jnp.where(match, 1.0, 0.0).astype(jnp.bfloat16)
             e = jnp.exp(st - top)
             est[t * 128 : t * 128 + 128, cols] = e
+            ebf[t * 128 : t * 128 + 128, cols] = e.astype(jnp.bfloat16)
             total += jnp.sum(e, axis=0, keepdims=True)
         stats[0, 0:1, cols] = top + jnp.log(total)
         stats[0, 1:2, cols] = positive
@@ -211,6 +217,14 @@
 
     for zi, xi in mates():
         send(f"S{zi}{xi}", stats.at[0], stats.at[SEEN[zi] * 2 + xi], at(xs[xi], zs[zi], y))
+    def products(slot):
+        rows = slice(slot * 256, slot * 256 + 256)
+        gif[rows, :] = lax.dot_general(ebf[:, rows], txt[...], TN, preferred_element_type=jnp.float32)
+        gis[rows, :] = lax.dot_general(chosen[:, rows], txt[0:512, :], TN, preferred_element_type=jnp.float32)
+
+    for slot in (3, 2, 1, 0):
+        products(slot)
+    settle(7)
     for zi, xi in mates():
         arrived(f"S{SEEN[zi]}{xi}", stats.at[zi * 2 + xi])
 
@@ -243,30 +257,32 @@
         rows = slice(slot * 128, (slot + count) * 128)
         gtf[rows, :] = lax.dot_general(wt[rows, :], img[...], NN, preferred_element_type=jnp.float32)
 
-    def put(slot, lo, more=()):
-        rows = slice(slot * 128 + lo, slot * 128 + lo + 64)
+    def put(slot, lo, more=(), n=64):
+        rows = slice(slot * 128 + lo, slot * 128 + lo + n)
         v = gtf[rows, :]
         for m in more:
             v = v + m.astype(jnp.float32)
         gtb[rows, :] = v.astype(jnp.bfloat16)
         return gtb.at[rows, :]
 
-    def send_q(slot, lo, more=()):
-        send(f"q{slot}{lo}", put(4 + slot, lo, more), rp.at[slot, lo : lo + 64, :], to_last)
-
-    def send_t(slot, lo, more=()):
+    def send_q(slot, lo, more=(), n=64):
+        send(f"q{slot}{lo}", put(4 + slot, lo, more, n), rp.at[slot, lo : lo + n, :], to_last)
+
+    def send_t(slot, lo, more=(), n=64):
         end, to = (1, to_ym) if slot == 1 else (0, to_yp)
-        more = [rp[slot, lo : lo + 64, :], *more]
-        send(f"t{slot}{lo}", put(slot, lo, more), rt2.at[end, lo : lo + 64, :], to)
+        more = [rp[slot, lo : lo + n, :], *more]
+        send(f"t{slot}{lo}", put(slot, lo, more, n), rt2.at[end, lo : lo + n, :], to)
 
     def gi_rows(slot, xi, lo=0, hi=128):
         return slice(slot * 256 + xi * 128 + lo, slot * 256 + xi * 128 + hi)
 
     def grad_image(slot):
-        rows = slice(slot * 256, slot * 256 + 256)
-        v = lax.dot_general(wt[:, rows], txt[...], TN, preferred_element_type=jnp.float32)
-        gif[rows, :] = v
-        gib[gi_rows(slot, 1), CA:1024] = v[128:256, CA:1024].astype(jnp.bfloat16)
+        for k in (2 * slot, 2 * slot + 1):
+            rows = slice(k * 128, k * 128 + 128)
+            for c in range(8):
+                cols = slice(c * 128, c * 128 + 128)
+                gif[rows, cols] = gif[rows, cols] * across[rows, :] - gis[rows, cols]
+        gib[gi_rows(slot, 1), CA:1024] = gif[gi_rows(slot, 1), CA:1024].astype(jnp.bfloat16)
 
     def send_b(slot):
         send(f"b{slot}", gib.at[gi_rows(slot, 1), CA:1024], rx.at[slot], to_px)
@@ -289,21 +305,24 @@
 
     weights(7)
     grad_text(7)
-    send("u0", put(7, 0), ru.at[0], to_yp)
-    send("u1", put(7, 64), ru.at[1], to_ym)
+    for lo in (0, 32):
+        send(f"u1{lo}", put(7, 64 + lo, n=32), ru.at[1, lo : lo + 32, :], to_ym)
+        send(f"u0{lo}", put(7, lo, n=32), ru.at[0, lo : lo + 32, :], to_yp)
     weights(5)
     weights(6)
     grad_text(5, 2)
     send_q(1, 0)
     send_q(2, 64)
-    for t in range(5):
-        weights(t)
+    for k in range(8):
+        rows = slice(k * 128, k * 128 + 128)
+        across[rows, :] = jnp.transpose(jnp.broadcast_to(factor[:, rows], (128, 128)))
     grad_image(3)
     send_a("a1", 3, 1, ra1.at[1], to_zm)
     send_a("a0", 3, 0, ra1.at[0], to_zp)
     send_b(3)
+    for t in range(5):
+        weights(t)
     grad_text(3, 2)
-    send_q(0, 0)
     send("t0", put(3, 0), rt1.at[0], to_yp)
     send("t1", put(3, 64), rt1.at[1], to_ym)
     grad_image(2)
@@ -312,10 +331,12 @@
     grad_image(1)
     send_a("a2", 1, 0, ra2.at[1, 0], to_zm)
     send_b(1)
-    arrived("u1", ru.at[1])
-    send_q(1, 64, [ru[1]])
-    arrived("u0", ru.at[0])
-    send_q(2, 0, [ru[0]])
+    for lo in (0, 32):
+        arrived(f"u1{lo}", ru.at[1, lo : lo + 32, :])
+        send_q(1, 64 + lo, [ru[1, lo : lo + 32, :]], 32)
+        arrived(f"u0{lo}", ru.at[0, lo : lo + 32, :])
+        send_q(2, lo, [ru[0, lo : lo + 32, :]], 32)
+    send_q(0, 0)
     send_q(0, 64)
     grad_image(0)
     send_b(0)
@@ -338,19 +359,24 @@
     send_t(2, 64)
     grad_text(0)
     arrived("t1", rt1.at[1])
-    arrived("q164", rp.at[1, 64:128, :])
-    send_t(1, 64, [rt1[1]])
+    arrived("q164", rp.at[1, 64:96, :])
+    send_t(1, 64, [rt1[1, 0:32, :]], 32)
+    arrived("t0", rt1.at[0])
+    arrived("q20", rp.at[2, 0:32, :])
+    send_t(2, 0, [rt1[0, 0:32, :]], 32)
     arrived("b2", rx.at[2])
     b_sum(2, 64, 128)
-    arrived("t0", rt1.at[0])
-    arrived("q20", rp.at[2, 0:64, :])
-    send_t(2, 0, [rt1[0]])
+    arrived("q196", rp.at[1, 96:128, :])
+    send_t(1, 96, [rt1[1, 32:64, :]], 32)
+    arrived("q232", rp.at[2, 32:64, :])
+    send_t(2, 32, [rt1[0, 32:64, :]], 32)
     arrived("a3", ra2.at[0, 1])
     arrived("a50", ra2.at[1, 1, 0:64, :])
     send_a("a60", 0, 1, ra3.at[0:64, :], to_px, [ra2[0, 1, 0:64, :], ra2[1, 1, 0:64, :]], 0, 64)
     arrived("b4", rb1.at[0])
     b_sum(2, 0, 64, rb1[0])
     send("b7", gib.at[gi_rows(2, 0), CA:1024], rb2.at[0], to_zp)
+    settle(14)
     arrived("b1", rx.at[1])
     b_sum(1, 0, 64)
     arrived("b5", rb1.at[1])
@@ -359,10 +385,13 @@
     arrived("a51", ra2.at[1, 1, 64:128, :])
     send_a("a61", 0, 1, ra3.at[64:128, :], to_px, [ra2[0, 1, 64:128, :], ra2[1, 1, 64:128, :]], 64, 128)
 
+    settle(5)
     for lo in (0, 64):
         arrived(f"q0{lo}", rp.at[0, lo : lo + 64, :])
-        arrived(f"t1{lo}", rt2.at[1, lo : lo + 64, :])
-        arrived(f"t2{lo}", rt2.at[0, lo : lo + 64, :])
+    for lo, n in ((0, 64), (64, 32), (96, 32)):
+        arrived(f"t1{lo}", rt2.at[1, lo : lo + n, :])
+    for lo, n in ((0, 32), (32, 32), (64, 64)):
+        arrived(f"t2{lo}", rt2.at[0, lo : lo + n, :])
     gt_ref[...] = (
         gtf[0:128, :] + rp[0].astype(jnp.float32) + rt2[0].astype(jnp.float32)
     )
@@ -382,9 +411,8 @@
         gif[0:128, 0:CA] + ra2[0, 0].astype(jnp.float32) + ra2[1, 0].astype(jnp.float32)
     )
     gi_last_ref[:, 0:CA] = ra3[...]
-    assert len(names) <= 96
-    for c in started:
-        c.wait_send()
+    assert len(names) <= 112
+    settle(0)
 
 
 def local(image, text, pair):
@@ -411,6 +439,10 @@
             pltpu.VMEM((1, 1024), f32),
             pltpu.VMEM((8, 2, 1024), f32),
             pltpu.VMEM((1024, 1024), bf16),
+            pltpu.VMEM((1024, 1024), bf16),
+            pltpu.VMEM((512, 1024), bf16),
+            pltpu.VMEM((1024, 128), f32),
+            pltpu.VMEM((1024, 1024), f32),
             pltpu.VMEM((1024, 1024), f32),
             pltpu.VMEM((1024, 1024), bf16),
             pltpu.VMEM((1024, 1024), f32),
@@ -425,8 +457,8 @@
             pltpu.VMEM((2, 128, CB), bf16),
             pltpu.VMEM((2, 64, 1024), bf16),
             pltpu.VMEM((2, 128, 1024), bf16),
-            pltpu.SemaphoreType.DMA((96,)),
-            pltpu.SemaphoreType.DMA((96,)),
+            pltpu.SemaphoreType.DMA((112,)),
+            pltpu.SemaphoreType.DMA((112,)),
             pltpu.SemaphoreType.DMA((2,)),
         ],
         compiler_params=pltpu.CompilerParams(

time: 50.6 us -> 50.2 us (level)
  no operation moved by 1% of the time
where the time goes in v5:
time: 50.2 us; the launch traced here: 49.5 us
  Pallas kernels  46.6 us (93%)
  local copies, waits for them, and re-layouts  1.16 us (2%)
  other arithmetic  1.1 us (2%)
  between operations  0.65 us (1%)
    pallas_call x1, Pallas kernels, local(): pl.pallas_call(kernel, out_shape=(jax.ShapeDtypeStruct((128,), f32), jax....  46.6 us
    unnamed x3, local copies, waits for them, and re-layouts  1.16 us
    add x1, other arithmetic, local(): grad_text + text_last.astype(f32)  1.1 us

profile of v5, /device:TPU:0, one launch (start us, length us, event | category | flops | bytes accessed | tf_op | source)
XLA Modules:
  0.0 49.5 jit_solution(13373937873116258844)
XLA Ops:
  0.6 0.0 copy-start
  0.6 0.6 %copy-done = s32[128]{0:T(128)S(1)} copy-done((s32[128]{0:T(128)S(1)}, s32[128]{0:T(128)}, u32[]{:S(2)}) %copy-start) | copy-done | bytes 536
  1.3 46.6 %shard_map.58 = (f32[128]{0:T(128)S(1)}, f32[128,1024]{1,0:T(8,128)S(1)}, f32[128,1024]{1,0:T(8,128)S(1)}, bf16[128,1024]{1,0:T(8,128)(2,1)S(1)}, bf16[128,1024]{1,0:T(8,128)(2,1)S(1)}) custom-call(f32[128,1024]{1,0:T(8,128)} %image_ref.1, f32[128,1024]{1,0:T(8,128)} %text_ref.1, s32[1,128]{1,0:T(1,128)S(1)} %bitcast.1), custom_call_target="tpu_custom_call" | custom-call | flops 6442450944 | bytes 2097152 | tf_op jit(solution)/shard_map/pallas_call | solution.py:423
  47.9 1.1 %convert_add_fusion = (f32[128,1024]{1,0:T(8,128)}, f32[128,1024]{1,0:T(8,128)}) fusion(f32[128,1024]{1,0:T(8,128)S(1)} %get-tuple-element.11, bf16[128,1024]{1,0:T(8,128)(2,1)S(1)} %get-tuple-element.12, f32[128,1024]{1,0:T(8,128)S(1)} %get-tuple-element.9, bf16[128,1024]{1,0:T(8,128)(2,1)S(1)} %get-tuple-element.10), kind=kLoop, calls=%fused_computation | loop fusion | flops 524288 | bytes 2621440 | tf_op jit(solution)/shard_map/add | solution.py:471
  49.0 0.5 %copy.7 = f32[128]{0:T(128)} copy(f32[128]{0:T(128)S(1)} %get-tuple-element.18) | data formatting | bytes 1024
Async XLA Ops:
  0.6 0.7 %copy-start = (s32[128]{0:T(128)S(1)}, s32[128]{0:T(128)}, u32[]{:S(2)}) copy-start(s32[128]{0:T(128)} %param.5) | copy-start | bytes 1540

commit v6 on v5

--- a/solution.py
+++ b/solution.py
@@ -386,30 +386,30 @@
     send_a("a61", 0, 1, ra3.at[64:128, :], to_px, [ra2[0, 1, 64:128, :], ra2[1, 1, 64:128, :]], 64, 128)
 
     settle(5)
+    arrived("b0", rx.at[0])
+    arrived("b7", rb2.at[0])
+    gi_ref[:, CA:1024] = (
+        gif[0:128, CA:1024] + rx[0].astype(jnp.float32) + rb2[0].astype(jnp.float32)
+    )
+    arrived("a2", ra2.at[1, 0])
+    arrived("a4", ra2.at[0, 0])
+    gi_ref[:, 0:CA] = (
+        gif[0:128, 0:CA] + ra2[0, 0].astype(jnp.float32) + ra2[1, 0].astype(jnp.float32)
+    )
     for lo in (0, 64):
         arrived(f"q0{lo}", rp.at[0, lo : lo + 64, :])
-    for lo, n in ((0, 64), (64, 32), (96, 32)):
-        arrived(f"t1{lo}", rt2.at[1, lo : lo + n, :])
-    for lo, n in ((0, 32), (32, 32), (64, 64)):
+    for lo, n in ((64, 64), (0, 32), (32, 32)):
         arrived(f"t2{lo}", rt2.at[0, lo : lo + n, :])
     gt_ref[...] = (
         gtf[0:128, :] + rp[0].astype(jnp.float32) + rt2[0].astype(jnp.float32)
     )
+    for lo, n in ((0, 64), (64, 32), (96, 32)):
+        arrived(f"t1{lo}", rt2.at[1, lo : lo + n, :])
     gt_last_ref[...] = rt2[1]
-    arrived("b0", rx.at[0])
     arrived("b6", rb2.at[1])
-    arrived("b7", rb2.at[0])
-    gi_ref[:, CA:1024] = (
-        gif[0:128, CA:1024] + rx[0].astype(jnp.float32) + rb2[0].astype(jnp.float32)
-    )
     gi_last_ref[:, CA:1024] = rb2[1]
-    arrived("a2", ra2.at[1, 0])
-    arrived("a4", ra2.at[0, 0])
     arrived("a60", ra3.at[0:64, :])
     arrived("a61", ra3.at[64:128, :])
-    gi_ref[:, 0:CA] = (
-        gif[0:128, 0:CA] + ra2[0, 0].astype(jnp.float32) + ra2[1, 0].astype(jnp.float32)
-    )
     gi_last_ref[:, 0:CA] = ra3[...]
     assert len(names) <= 112
     settle(0)

time: 50.2 us -> 50.1 us (level)
  no operation moved by 1% of the time
where the time goes in v6:
time: 50.1 us; the launch traced here: 49.4 us
  Pallas kernels  46.5 us (93%)
  local copies, waits for them, and re-layouts  1.16 us (2%)
  other arithmetic  1.1 us (2%)
  between operations  0.65 us (1%)
    pallas_call x1, Pallas kernels, local(): pl.pallas_call(kernel, out_shape=(jax.ShapeDtypeStruct((128,), f32), jax....  46.5 us
    unnamed x3, local copies, waits for them, and re-layouts  1.16 us
    add x1, other arithmetic, local(): grad_text + text_last.astype(f32)  1.1 us

profile of v6, /device:TPU:0, one launch (start us, length us, event | category | flops | bytes accessed | tf_op | source)
XLA Modules:
  0.0 49.4 jit_solution(1018808295521973503)
XLA Ops:
  0.6 0.0 copy-start
  0.6 0.6 %copy-done = s32[128]{0:T(128)S(1)} copy-done((s32[128]{0:T(128)S(1)}, s32[128]{0:T(128)}, u32[]{:S(2)}) %copy-start) | copy-done | bytes 536
  1.3 46.5 %shard_map.58 = (f32[128]{0:T(128)S(1)}, f32[128,1024]{1,0:T(8,128)S(1)}, f32[128,1024]{1,0:T(8,128)S(1)}, bf16[128,1024]{1,0:T(8,128)(2,1)S(1)}, bf16[128,1024]{1,0:T(8,128)(2,1)S(1)}) custom-call(f32[128,1024]{1,0:T(8,128)} %image_ref.1, f32[128,1024]{1,0:T(8,128)} %text_ref.1, s32[1,128]{1,0:T(1,128)S(1)} %bitcast.1), custom_call_target="tpu_custom_call" | custom-call | flops 6442450944 | bytes 2097152 | tf_op jit(solution)/shard_map/pallas_call | solution.py:423
  47.8 1.1 %convert_add_fusion = (f32[128,1024]{1,0:T(8,128)}, f32[128,1024]{1,0:T(8,128)}) fusion(f32[128,1024]{1,0:T(8,128)S(1)} %get-tuple-element.11, bf16[128,1024]{1,0:T(8,128)(2,1)S(1)} %get-tuple-element.12, f32[128,1024]{1,0:T(8,128)S(1)} %get-tuple-element.9, bf16[128,1024]{1,0:T(8,128)(2,1)S(1)} %get-tuple-element.10), kind=kLoop, calls=%fused_computation | loop fusion | flops 524288 | bytes 2621440 | tf_op jit(solution)/shard_map/add | solution.py:471
  48.9 0.5 %copy.7 = f32[128]{0:T(128)} copy(f32[128]{0:T(128)S(1)} %get-tuple-element.18) | data formatting | bytes 1024
Async XLA Ops:
  0.6 0.7 %copy-start = (s32[128]{0:T(128)S(1)}, s32[128]{0:T(128)}, u32[]{:S(2)}) copy-start(s32[128]{0:T(128)} %param.5) | copy-start | bytes 1540

commit v7 on v6

--- a/solution.py
+++ b/solution.py
@@ -60,8 +60,6 @@
     pairs[:, 0:128] = pair_ref[...]
     text_in.wait()
     txt[0:128, :] = gtf[0:128, :].astype(jnp.bfloat16)
-    image_in.wait()
-    img[0:128, :] = gif[0:128, :].astype(jnp.bfloat16)
 
     pl.semaphore_wait(barrier, len(peers))
 
@@ -98,10 +96,12 @@
 
     send("T0a", T(0, 0, 64), T(1, 0, 64), to_yp)
     send("T1b", T(0, 64, 128), T(2, 64, 128), to_ym)
+    send("P0", T(0), T(4), to_next)
+    image_in.wait()
+    img[0:128, :] = gif[0:128, :].astype(jnp.bfloat16)
     send("B0", B(0, 0), B(1, 0), to_zp)
     send("B1", B(0, 0), B(2, 0), to_zm)
     send("A0", A(0, 0), A(0, 1), to_px)
-    send("P0", T(0), T(4), to_next)
     def chunk(zi, xi):
         return slice(zi * 256 + xi * 128, zi * 256 + xi * 128 + 128)
 

time: 50.1 us -> 50.2 us (level)
  no operation moved by 1% of the time
where the time goes in v7:
time: 50.2 us; the launch traced here: 49.5 us
  Pallas kernels  46.5 us (93%)
  local copies, waits for them, and re-layouts  1.16 us (2%)
  other arithmetic  1.1 us (2%)
  between operations  0.65 us (1%)
    pallas_call x1, Pallas kernels, local(): pl.pallas_call(kernel, out_shape=(jax.ShapeDtypeStruct((128,), f32), jax....  46.5 us
    unnamed x3, local copies, waits for them, and re-layouts  1.16 us
    add x1, other arithmetic, local(): grad_text + text_last.astype(f32)  1.1 us

profile of v7, /device:TPU:0, one launch (start us, length us, event | category | flops | bytes accessed | tf_op | source)
XLA Modules:
  0.0 49.5 jit_solution(16990176657418659360)
XLA Ops:
  0.6 0.0 copy-start
  0.6 0.6 %copy-done = s32[128]{0:T(128)S(1)} copy-done((s32[128]{0:T(128)S(1)}, s32[128]{0:T(128)}, u32[]{:S(2)}) %copy-start) | copy-done | bytes 536
  1.3 46.5 %shard_map.58 = (f32[128]{0:T(128)S(1)}, f32[128,1024]{1,0:T(8,128)S(1)}, f32[128,1024]{1,0:T(8,128)S(1)}, bf16[128,1024]{1,0:T(8,128)(2,1)S(1)}, bf16[128,1024]{1,0:T(8,128)(2,1)S(1)}) custom-call(f32[128,1024]{1,0:T(8,128)} %image_ref.1, f32[128,1024]{1,0:T(8,128)} %text_ref.1, s32[1,128]{1,0:T(1,128)S(1)} %bitcast.1), custom_call_target="tpu_custom_call" | custom-call | flops 6442450944 | bytes 2097152 | tf_op jit(solution)/shard_map/pallas_call | solution.py:423
  47.8 1.1 %convert_add_fusion = (f32[128,1024]{1,0:T(8,128)}, f32[128,1024]{1,0:T(8,128)}) fusion(f32[128,1024]{1,0:T(8,128)S(1)} %get-tuple-element.11, bf16[128,1024]{1,0:T(8,128)(2,1)S(1)} %get-tuple-element.12, f32[128,1024]{1,0:T(8,128)S(1)} %get-tuple-element.9, bf16[128,1024]{1,0:T(8,128)(2,1)S(1)} %get-tuple-element.10), kind=kLoop, calls=%fused_computation | loop fusion | flops 524288 | bytes 2621440 | tf_op jit(solution)/shard_map/add | solution.py:471
  48.9 0.5 %copy.7 = f32[128]{0:T(128)} copy(f32[128]{0:T(128)S(1)} %get-tuple-element.18) | data formatting | bytes 1024
Async XLA Ops:
  0.6 0.7 %copy-start = (s32[128]{0:T(128)S(1)}, s32[128]{0:T(128)}, u32[]{:S(2)}) copy-start(s32[128]{0:T(128)} %param.5) | copy-start | bytes 1540
